TPU v7x, 32 devices: a whole 2x2x4 slice. The times are simulated.
32 devices in a mesh: dp: 2 (over y), row: 4 (over z), col: 4 (over x, core).
Axes of the slice: x: 2, y: 2, z: 4, core: 2. Of those that a mesh axis runs over, the one named last changes fastest.
Arguments:
- tokens: bfloat16 [2048, 1024], P(('dp', 'row')), may hold values from -6 to 6
- cotangent: bfloat16 [2048, 1024], P(('dp', 'row')), may hold values from -6 to 6
- norm_in: float32 [1024], replicated, may hold values from 0.5 to 1.5
- z_weight: bfloat16 [1024, 1536], P(('dp', 'row'), 'col'), may hold values from -0.1875 to 0.1875
- x_weight: bfloat16 [1024, 1536], P(('dp', 'row'), 'col'), may hold values from -0.1875 to 0.1875
- dt_weight: bfloat16 [1024, 24], P(('dp', 'row'), 'col'), may hold values from -0.1875 to 0.1875
- q_weight: bfloat16 [1024, 512], P(('dp', 'row'), 'col'), may hold values from -0.1875 to 0.1875
- bc_weight: bfloat16 [1024, 256], P(('dp', 'row')), may hold values from -0.1875 to 0.1875
- key_value_weight: bfloat16 [1024, 256], P(('dp', 'row')), may hold values from -0.1875 to 0.1875
- conv_x: float32 [4, 1536], P(None, 'col'), may hold values from -0.5 to 0.5
- conv_bc: float32 [4, 256], replicated, may hold values from -0.5 to 0.5
- dt_bias: float32 [24], P('col'), may hold values from -7 to -2.3
- a_log: float32 [24], P('col'), may hold values from 0 to 2.77
- d_skip: float32 [24], P('col'), may hold values from 0.5 to 1.5
- gate_gain: float32 [1536], P('col'), may hold values from 0.5 to 1.5
- mamba_weight: bfloat16 [1536, 1024], P('col', ('dp', 'row')), may hold values from -0.15625 to 0.15625
- attn_weight: bfloat16 [512, 1024], P('col', ('dp', 'row')), may hold values from -1 to 1
- norm_mid: float32 [1024], replicated, may hold values from 0.5 to 1.5
- gate_weight: bfloat16 [1024, 2048], P(('dp', 'row'), 'col'), may hold values from -0.1875 to 0.1875
- up_weight: bfloat16 [1024, 2048], P(('dp', 'row'), 'col'), may hold values from -0.1875 to 0.1875
- down_weight: bfloat16 [2048, 1024], P('col', ('dp', 'row')), may hold values from -0.125 to 0.125
Outputs:
- layer_out: bfloat16 [2048, 1024], P(('dp', 'row'))
- grad_tokens: float32 [2048, 1024], P(('dp', 'row'))
- grad_norm_in: float32 [1024], replicated
- grad_z_weight: float32 [1024, 1536], P(('dp', 'row'), 'col')
- grad_x_weight: float32 [1024, 1536], P(('dp', 'row'), 'col')
- grad_dt_weight: float32 [1024, 24], P(('dp', 'row'), 'col')
- grad_q_weight: float32 [1024, 512], P(('dp', 'row'), 'col')
- grad_bc_weight: float32 [1024, 256], P(('dp', 'row'))
- grad_kv_weight: float32 [1024, 256], P(('dp', 'row'))
- grad_conv_x: float32 [4, 1536], P(None, 'col')
- grad_conv_bc: float32 [4, 256], replicated
- grad_dt_bias: float32 [24], P('col')
- grad_a_log: float32 [24], P('col')
- grad_d_skip: float32 [24], P('col')
- grad_gate_gain: float32 [1536], P('col')
- grad_mamba_weight: float32 [1536, 1024], P('col', ('dp', 'row'))
- grad_attn_weight: float32 [512, 1024], P('col', ('dp', 'row'))
- grad_norm_mid: float32 [1024], replicated
- grad_gate_weight: float32 [1024, 2048], P(('dp', 'row'), 'col')
- grad_up_weight: float32 [1024, 2048], P(('dp', 'row'), 'col')
- grad_down_weight: float32 [2048, 1024], P('col', ('dp', 'row'))
All inputs are finite; a program needn't handle non-finite values.
Results may differ from a plain program's by a relative error of at most 0.03.
Values may be sent and summed in bfloat16 or wider, within the bound.
No kernel may reach another device: no remote copies, remote signals or barrier semaphores. Data moves between devices by JAX's collectives and lax.ppermute only.
A program may use at most 128 MiB of HBM per device.

v0:
```python
from functools import partial

import jax
import jax.numpy as jnp
from jax import lax
from jax.experimental import pallas as pl
from jax.experimental.pallas import tpu as pltpu
from jax.sharding import PartitionSpec as P

HM = 24
PM = 64
NS = 128
KC = 4
QUERY_HEADS = 8
KEY_HEADS = 2
HEAD_DIM = 64
HALO = 16
LANES = 128

EPSILON = 1e-05
ROPE_BASE = 100000000000.0
NEG_LARGE = -1e30
HIGHEST = lax.Precision.HIGHEST
F32 = jnp.float32
BF16 = jnp.bfloat16


def mm(a, b, precision=None):
    return lax.dot_general(
        a, b, (((1,), (0,)), ((), ())), precision=precision, preferred_element_type=F32
    )


def mm_nt(a, b, precision=None):
    return lax.dot_general(
        a, b, (((1,), (1,)), ((), ())), precision=precision, preferred_element_type=F32
    )


def mm_tn(a, b, precision=None):
    return lax.dot_general(
        a, b, (((0,), (0,)), ((), ())), precision=precision, preferred_element_type=F32
    )


def low(v):
    return v.astype(BF16)


def sigmoid(v):
    return 1.0 / (1.0 + jnp.exp(-v))


def softplus(v):
    return jnp.maximum(v, 0.0) + jnp.log1p(jnp.exp(-jnp.abs(v)))


def head_lanes(heads):
    head = lax.broadcasted_iota(jnp.int32, (LANES, heads * PM), 0)
    column = lax.broadcasted_iota(jnp.int32, (LANES, heads * PM), 1)
    return ((column >= head * PM) & (column < head * PM + PM)).astype(F32)


def lower_triangle(size):
    later = lax.broadcasted_iota(jnp.int32, (size, size), 0)
    earlier = lax.broadcasted_iota(jnp.int32, (size, size), 1)
    return later >= earlier


def split_pair(pair):
    first = lax.broadcasted_iota(jnp.int32, pair.shape, 1) < PM
    zero = jnp.zeros_like(pair)
    return jnp.concatenate([jnp.where(first, pair, zero), jnp.where(first, zero, pair)], axis=0)


def kernel_call(body, outs, cost, scalars, *operands, keep=False):
    flops, traffic, exps = cost
    flat, in_specs, scratch, plan = [], [], [], []
    if scalars is not None:
        flat.append(scalars)
        in_specs.append(pl.BlockSpec(memory_space=pltpu.SMEM))
    for operand in operands:
        parts = operand if isinstance(operand, list) else [operand]
        plan.append((len(flat), len(parts), isinstance(operand, list)))
        flat += parts
        space = pltpu.HBM if isinstance(operand, list) else pltpu.VMEM
        in_specs += [pl.BlockSpec(memory_space=space)] * len(parts)
        if isinstance(operand, list):
            whole = (sum(v.shape[0] for v in parts), parts[0].shape[1])
            scratch.append(pltpu.VMEM(whole, parts[0].dtype))
            last = (whole, parts[0].dtype)
    if keep:
        scratch.pop()
        outs = tuple(outs) + (last,)
    copied = sum(n for _, n, outside in plan if outside)
    if copied:
        scratch.append(pltpu.SemaphoreType.DMA((copied,)))

    def run(*refs):
        ins, results, held = refs[: len(flat)], refs[len(flat) : len(flat) + len(outs)], refs[len(flat) + len(outs) :]
        views = [ins[0]] if scalars is not None else []
        copies, taken = [], 0
        for start, n, outside in plan:
            if not outside:
                views.append(ins[start])
                continue
            target = results[-1] if keep and taken == len(scratch) - 1 else held[taken]
            taken += 1
            views.append(target)
            for i in range(n):
                size = ins[start + i].shape[0]
                place = target if n == 1 else target.at[lanes_of(ins[0], i, size), :]
                copies.append(pltpu.make_async_copy(ins[start + i], place, held[-1].at[len(copies)]))
        for c in copies:
            c.start()
        for c in copies:
            c.wait()
        body(*views, *(results[:-1] if keep else results))

    return pl.pallas_call(
        run,
        out_shape=tuple(jax.ShapeDtypeStruct(s, d) for s, d in outs),
        in_specs=in_specs,
        out_specs=tuple(pl.BlockSpec(memory_space=pltpu.VMEM) for _ in outs),
        scratch_shapes=scratch,
        compiler_params=pltpu.CompilerParams(vmem_limit_bytes=24 * 1024 * 1024),
        cost_estimate=pl.CostEstimate(flops=flops, bytes_accessed=traffic, transcendentals=exps),
    )(*flat)


def lanes_of(scalars, p, size):
    return pl.ds(pl.multiple_of(scalars[p] * size, size), size)


def rows_half(parity, rows, own):
    half = rows // 2
    return pl.ds(pl.multiple_of((parity if own else 1 - parity) * half, half), half)


def halves_to_sum(parity, full_ref, keep_ref, give_ref):
    rows = full_ref.shape[0]
    keep_ref[...] = full_ref[rows_half(parity, rows, True), :]
    give_ref[...] = low(full_ref[rows_half(parity, rows, False), :])


def halves_joined(parity, total_ref, other_ref, full_ref):
    rows = full_ref.shape[0]
    full_ref[rows_half(parity, rows, True), :] = total_ref[...].astype(F32)
    full_ref[rows_half(parity, rows, False), :] = other_ref[...].astype(F32)


def pack_rows(v, width):
    count = width // HEAD_DIM
    chunk = packed_rows(v.shape[0], width)
    pieces = []
    for i in range(count):
        piece = v[i * chunk : min((i + 1) * chunk, v.shape[0])]
        if piece.shape[0] < chunk:
            piece = jnp.concatenate([piece, jnp.zeros((chunk - piece.shape[0], HEAD_DIM), v.dtype)], axis=0)
        pieces.append(piece)
    return jnp.concatenate(pieces, axis=1)


def packed_rows(rows, width):
    count = width // HEAD_DIM
    return -(-rows // (16 * count)) * 16


def unpack_rows(v, rows):
    count = v.shape[1] // HEAD_DIM
    return jnp.concatenate([v[:, i * HEAD_DIM : (i + 1) * HEAD_DIM] for i in range(count)], axis=0)[:rows]


def token_sums(v):
    return mm_nt(jnp.ones((8, v.shape[1]), F32), v, HIGHEST)


def as_column(v):
    return jnp.transpose(v)[:, :1]


def scan_local(
    heads, scalars, hidden_ref, taps_ref, par_ref, skip_ref, cos_ref, sin_ref, w_ref,
    y_ref, msg_ref, proj_ref, x_ref, bc_ref, slope_ref, cum_ref, step_ref,
):
    width = heads * PM
    conv_width = width + 2 * NS
    rows = y_ref.shape[0]
    proj = low(mm(hidden_ref[...], w_ref[...]))
    proj_ref[...] = proj
    ext = proj[:, :conv_width].astype(F32)
    pre = taps_ref[KC - 1 : KC, :] * ext[HALO:]
    for k in range(KC - 1):
        pre = pre + taps_ref[k : k + 1, :] * pltpu.roll(ext, KC - 1 - k, 0)[HALO:]
    sig = sigmoid(pre)
    conv_out = pre * sig
    slope_ref[...] = sig * (1.0 + pre * (1.0 - sig))
    x = conv_out[:, :width]
    x_ref[...] = x
    bc_ref[...] = conv_out[:, width:]
    b_map = low(conv_out[:, width : width + NS])
    c_map = low(conv_out[:, width + NS :])
    raw = proj[HALO:, conv_width + LANES :].astype(F32) + par_ref[0:1, :]
    lane = lax.broadcasted_iota(jnp.int32, raw.shape, 1)
    step = jnp.where(lane < heads, softplus(raw), 0.0)
    step_ref[...] = step
    causal = lower_triangle(rows)
    cum = mm(causal.astype(F32), step * par_ref[1:2, :], HIGHEST)
    cum_ref[...] = cum
    spread = head_lanes(heads)
    last = cum[rows - 1 : rows, :]
    tail = mm(jnp.exp(last - cum) * step, spread, HIGHEST)
    msg_ref[:NS, :] = low(mm_tn(b_map, low(x * tail)))
    decay = mm(jnp.exp(jnp.broadcast_to(last, (HALO, LANES))), spread, HIGHEST)
    coarse = low(decay)
    fine = low(decay - coarse.astype(F32))
    place = lax.broadcasted_iota(jnp.int32, decay.shape, 0)
    msg_ref[NS : NS + HALO, :] = low(jnp.where(place == 0, coarse.astype(F32), fine.astype(F32)))
    kv = proj[HALO:, conv_width : conv_width + LANES]
    turned = mm(kv, low(quarter_turn(LANES)))
    kv = low(kv.astype(F32) * cos_ref[...] + turned * sin_ref[...])
    part = packed_rows(rows, width)
    at = NS + HALO
    msg_ref[at : at + part, :] = pack_rows(kv[:, :HEAD_DIM], width)
    msg_ref[at + part : at + 2 * part, :] = pack_rows(kv[:, HEAD_DIM:], width)
    cum_t = jnp.transpose(cum)
    step_t = jnp.transpose(step)
    meet = jnp.where(causal, mm_nt(c_map, b_map), 0.0)
    for pair in range(heads // 2):
        mixing = []
        for h in (2 * pair, 2 * pair + 1):
            gap = jnp.minimum(cum[:, h : h + 1] - cum_t[h : h + 1, :], 0.0)
            mixing.append(low(meet * jnp.exp(gap) * step_t[h : h + 1, :]))
        lanes = slice(pair * LANES, (pair + 1) * LANES)
        y_ref[:, lanes] = (
            mm(jnp.concatenate(mixing, axis=1), split_pair(low(x[:, lanes])))
            + skip_ref[0:1, lanes] * x[:, lanes]
        )


def scan_back_local(
    heads, dy_ref, x_ref, bc_ref, cum_ref, step_ref, carried_ref, state_ref, skip_ref,
    dx_ref, dbc_ref, dcum_ref, dstep_ref, dskip_ref,
):
    rows = dy_ref.shape[0]
    dy = dy_ref[...]
    x = x_ref[...]
    b_map = low(bc_ref[:, :NS])
    c_map = low(bc_ref[:, NS:])
    cum = cum_ref[...]
    step = step_ref[...]
    cum_t = jnp.transpose(cum)
    step_t = jnp.transpose(step)
    causal = lower_triangle(rows)
    meet = jnp.where(causal, mm_nt(c_map, b_map), 0.0)
    lane = lax.broadcasted_iota(jnp.int32, (rows, LANES), 1)
    dmeet = jnp.zeros((rows, rows), F32)
    row_part = jnp.zeros((rows, LANES), F32)
    column_sums = []
    for pair in range(heads // 2):
        lanes = slice(pair * LANES, (pair + 1) * LANES)
        x_pair = low(x[:, lanes])
        dy_split = split_pair(low(dy[:, lanes]))
        dmix_both = mm_nt(dy_split, x_pair)
        mixing = []
        for i in range(2):
            h = 2 * pair + i
            dmix = dmix_both[i * rows : (i + 1) * rows]
            gap = jnp.minimum(cum[:, h : h + 1] - cum_t[h : h + 1, :], 0.0)
            decay = jnp.where(causal, jnp.exp(gap), 0.0)
            row_step = step_t[h : h + 1, :]
            decay_step = decay * row_step
            dmeet = dmeet + dmix * decay_step
            mixing.append(low(meet * decay_step))
            ratio = dmix * meet * decay
            column_sums.append(jnp.sum(ratio, axis=0, keepdims=True))
            row_sum = jnp.sum(ratio * row_step, axis=1, keepdims=True)
            row_part = row_part + jnp.where(lane == h, row_sum, 0.0)
        dx_ref[:, lanes] = (
            mm_tn(jnp.concatenate(mixing, axis=0), dy_split) + skip_ref[0:1, lanes] * dy[:, lanes]
        )
    column_sums.append(jnp.zeros((LANES - heads, rows), F32))
    dstep = jnp.transpose(jnp.concatenate(column_sums, axis=0))
    dstep_ref[...] = dstep
    spread = head_lanes(heads)
    weighted = dy * mm(jnp.exp(cum), spread, HIGHEST)
    dcum_ref[...] = row_part - dstep * step + mm_nt(weighted * carried_ref[...], spread, HIGHEST)
    dmeet_low = low(dmeet)
    dbc_ref[:, :NS] = mm_tn(dmeet_low, c_map)
    dbc_ref[:, NS:] = mm(dmeet_low, b_map) + mm_nt(low(weighted), low(state_ref[...]))
    dskip = jnp.broadcast_to(jnp.sum(dy * x, axis=0, keepdims=True), (8, dy.shape[1]))
    dskip_ref[...] = mm_nt(dskip, spread, HIGHEST)


def scan_back_end(
    heads, count, *refs
):
    got = refs[:count]
    (
        state_ref, x_ref, bc_ref, cum_ref, step_ref, dx_ref, dbc_ref, dcum_ref, dstep_ref, slope_ref,
        proj_ref, par_ref, dkv_ref, cos_ref, sin_ref,
        dpre_ref, first_ref, ddt_ref, dkv_out_ref, small_ref, dtaps_ref,
    ) = refs[count:]
    width = heads * PM
    conv_width = width + 2 * NS
    rows = x_ref.shape[0]
    part = packed_rows(rows, width)
    dkv = dkv_ref[...]
    dstate = jnp.zeros((NS, width), F32)
    for g in got:
        dstate = dstate + g[:NS, :].astype(F32)
        key = unpack_rows(g[NS : NS + part, :], rows)
        value = unpack_rows(g[NS + part : NS + 2 * part, :], rows)
        dkv = dkv + jnp.concatenate([key, value], axis=1).astype(F32)
    turned = mm(dkv, quarter_turn(LANES), HIGHEST)
    dkv_out_ref[...] = low(dkv * cos_ref[...] - turned * sin_ref[...])
    x = x_ref[...]
    b_map = low(bc_ref[:, :NS])
    cum = cum_ref[...]
    step = step_ref[...]
    spread = head_lanes(heads)
    last = cum[rows - 1 : rows, :]
    fade = jnp.exp(last - cum)
    tail = fade * step
    wide_tail = mm(tail, spread, HIGHEST)
    dstate_low = low(dstate)
    reach = mm(b_map, dstate_low)
    dx = dx_ref[...] + wide_tail * reach
    db = dbc_ref[:, :NS] + mm_nt(low(x * wide_tail), dstate_low)
    value = mm_nt(x * reach, spread, HIGHEST)
    total = jnp.sum(dstate * state_ref[...], axis=0, keepdims=True)
    dtotal = mm_nt(jnp.broadcast_to(total, (8, width)), spread, HIGHEST)[0:1, :]
    held = tail * value
    at_end = jnp.exp(last) * dtotal + jnp.sum(held, axis=0, keepdims=True)
    upper = jnp.where(lower_triangle(rows), 1.0, 0.0)
    drate = mm_tn(upper, dcum_ref[...] - held, HIGHEST) + at_end
    dstep = dstep_ref[...] + fade * value + drate * par_ref[1:2, :]
    raw = proj_ref[HALO:, conv_width + LANES :].astype(F32) + par_ref[0:1, :]
    lane = lax.broadcasted_iota(jnp.int32, raw.shape, 1)
    ddt = jnp.where(lane < heads, dstep * sigmoid(raw), 0.0)
    ddt_ref[...] = low(ddt)
    dbias = jnp.sum(ddt, axis=0, keepdims=True)
    dlog = jnp.sum(drate * step, axis=0, keepdims=True) * par_ref[1:2, :]
    place = lax.broadcasted_iota(jnp.int32, (8, LANES), 0)
    small_ref[...] = jnp.where(place == 0, dbias, jnp.where(place == 1, dlog, 0.0))
    dpre = jnp.concatenate([dx, db, dbc_ref[:, NS:]], axis=1) * slope_ref[...]
    dpre_ref[...] = dpre
    first_ref[...] = dpre[:8]
    ext = proj_ref[:, :conv_width].astype(F32)
    sums = [
        jnp.sum(dpre * (pltpu.roll(ext, KC - 1 - k, 0) if k < KC - 1 else ext)[HALO:], axis=0, keepdims=True)
        for k in range(KC)
    ]
    dtaps_ref[...] = jnp.concatenate(sums + [jnp.zeros((8 - KC, conv_width), F32)], axis=0)


def heads_to_rows(v):
    return jnp.concatenate([v[:, i * HEAD_DIM : (i + 1) * HEAD_DIM] for i in range(v.shape[1] // HEAD_DIM)], axis=0)


def rows_to_heads(v, count):
    rows = v.shape[0] // count
    return jnp.concatenate([v[i * rows : (i + 1) * rows] for i in range(count)], axis=1)


def quarter_turn(width):
    source = lax.broadcasted_iota(jnp.int32, (width, width), 0)
    target = lax.broadcasted_iota(jnp.int32, (width, width), 1)
    half = HEAD_DIM // 2
    upper = (target & (HEAD_DIM - 1)) >= half
    from_first = jnp.where(source == target - half, 1.0, 0.0)
    from_second = jnp.where(source == target + half, -1.0, 0.0)
    return jnp.where(upper, from_first, from_second)


def mix_tokens(
    heads, count, scalars, own_ref, *refs
):
    msgs = refs[:count]
    (
        y_ref, cum_ref, bc_ref, zq_ref, cos_ref, sin_ref,
        out_ref, probs_ref, query_ref, key_ref, value_ref, state_ref, carried_ref, y_out_ref, gated_ref, sums_ref,
    ) = refs[count:]
    row = scalars[scalars.shape[0] - 1]
    rows, width = y_ref.shape
    at = NS + HALO
    part = packed_rows(rows, width)
    everyone = (own_ref,) + msgs
    key = jnp.concatenate([unpack_rows(m[at : at + part, :], rows) for m in everyone], axis=0)
    value = jnp.concatenate([unpack_rows(m[at + part : at + 2 * part, :], rows) for m in everyone], axis=0)
    key_ref[...] = key
    value_ref[...] = value

    state = msgs[-1][:NS, :].astype(F32)
    for m in reversed(msgs[:-1]):
        decay = m[NS : NS + HALO, :].astype(F32)
        state = m[:NS, :].astype(F32) + (decay[0:1, :] + decay[1:2, :]) * state
    state_ref[...] = state
    carried = mm(low(bc_ref[:, NS:]), low(state))
    carried_ref[...] = carried
    y = y_ref[...] + mm(jnp.exp(cum_ref[...]), head_lanes(heads), HIGHEST) * carried
    y_out_ref[...] = y
    z = zq_ref[:, :width].astype(F32)
    gated = y * (z * sigmoid(z))
    gated_ref[...] = gated
    sums_ref[...] = token_sums(gated * gated)

    q = zq_ref[:, width:]
    q_heads = q.shape[1] // HEAD_DIM
    turned = mm(q, low(quarter_turn(q.shape[1])))
    query = heads_to_rows(low(q.astype(F32) * cos_ref[...] + turned * sin_ref[...]))
    query_ref[...] = query
    scores = mm_nt(query, key) * (HEAD_DIM ** (-0.5))
    place = lax.broadcasted_iota(jnp.int32, scores.shape, 0)
    column = lax.broadcasted_iota(jnp.int32, scores.shape, 1)
    place = place & (rows - 1)
    limit = jnp.where(column < rows, place, (row + 1) * rows - 1)
    scores = jnp.where(column <= limit, scores, NEG_LARGE)
    exponent = jnp.exp(scores - jnp.max(scores, axis=1, keepdims=True))
    probs = low(exponent * (1.0 / jnp.sum(exponent, axis=1, keepdims=True)))
    probs_ref[...] = probs
    out_ref[...] = low(rows_to_heads(mm(probs, value), q_heads))


def attend_back(grad_ref, probs_ref, query_ref, cos_ref, sin_ref, key_ref, value_ref, dq_ref, dkv_ref, *sent):
    count = grad_ref.shape[1] // HEAD_DIM
    rows = dkv_ref.shape[0]
    scale = HEAD_DIM ** (-0.5)
    grad = heads_to_rows(grad_ref[...])
    probs_low = probs_ref[...]
    probs = probs_low.astype(F32)
    dprobs = mm_nt(grad, value_ref[...])
    delta = jnp.sum(probs * dprobs, axis=1, keepdims=True)
    dscores = low(probs * (dprobs - delta))
    dquery = rows_to_heads(mm(dscores, key_ref[...]), count) * scale
    turned = mm(dquery, quarter_turn(dquery.shape[1]), HIGHEST)
    dq_ref[...] = low(dquery * cos_ref[...] - turned * sin_ref[...])
    dkey = mm_tn(dscores, query_ref[...]) * scale
    dvalue = mm_tn(probs_low, grad)
    dkv_ref[...] = jnp.concatenate([dkey[:rows], dvalue[:rows]], axis=1)
    for j, out in enumerate(sent):
        at = slice((j + 1) * rows, (j + 2) * rows)
        part = packed_rows(rows, out.shape[1])
        out[:part, :] = pack_rows(low(dkey[at]), out.shape[1])
        out[part:, :] = pack_rows(low(dvalue[at]), out.shape[1])


def project(scalars, hidden_ref, w_ref, out_ref):
    out_ref[...] = low(mm(hidden_ref[...], w_ref[:, : out_ref.shape[1]]))


def mix_out(
    total_heads, scalars, sums_ref, gated_ref, gain_ref, attn_ref, w_ref, normed_ref, keep_ref, give_ref, full_ref
):
    parity = scalars[scalars.shape[0] - 2]
    inv = as_column(lax.rsqrt(sums_ref[...] / (total_heads * PM) + EPSILON))
    normed = low(gated_ref[...] * inv * gain_ref[...])
    normed_ref[...] = normed
    act = jnp.concatenate([normed, attn_ref[...]], axis=1)
    full_ref[...] = mm_nt(act, w_ref[:, w_ref.shape[1] - act.shape[1] :])
    halves_to_sum(parity, full_ref, keep_ref, give_ref)


def feed_forward(
    scalars, total_ref, other_ref, tokens_ref, cot_ref, gain_ref, w_ref,
    middle_ref, hidden_ref, dgu_ref, swiglu_ref, keep_ref, give_ref, out_keep_ref, out_give_ref, full_ref,
):
    parity = scalars[scalars.shape[0] - 2]
    halves_joined(parity, total_ref, other_ref, full_ref)
    middle = tokens_ref[...].astype(F32) + full_ref[...]
    middle_ref[...] = middle
    inv = lax.rsqrt(jnp.mean(middle * middle, axis=-1, keepdims=True) + EPSILON)
    hidden_ref[...] = low(middle * inv * gain_ref[...])
    width = swiglu_ref.shape[1]
    gate_up = low(mm(hidden_ref[...], w_ref[:, : 2 * width])).astype(F32)
    gate, up = gate_up[:, :width], gate_up[:, width:]
    sig = sigmoid(gate)
    swish = gate * sig
    swiglu = low(swish * up)
    swiglu_ref[...] = swiglu
    grad = mm(cot_ref[...], w_ref[:, 2 * width :])
    dgate = low(grad * up * sig * (1.0 + gate * (1.0 - sig)))
    dup = low(grad * swish)
    dgu = jnp.concatenate([dgate, dup], axis=1)
    dgu_ref[...] = dgu
    full_ref[...] = mm_nt(dgu, w_ref[:, : 2 * width])
    halves_to_sum(parity, full_ref, keep_ref, give_ref)
    full_ref[...] = mm_nt(swiglu, w_ref[:, 2 * width :])
    halves_to_sum(parity, full_ref, out_keep_ref, out_give_ref)


def weight_products(count, scalars, *refs):
    outs = 1 if count == 1 else 2
    pairs, results = refs[:-outs], refs[-outs:]
    size = pairs[0].shape[1] // count
    for p in range(count):
        out = results[p * outs // count]
        rows = slice((p % (count // outs)) * size, (p % (count // outs) + 1) * size)
        at = 0
        for left, right in zip(pairs[0::2], pairs[1::2]):
            out[rows, at : at + right.shape[1]] = low(mm_tn(left[:, lanes_of(scalars, p, size)], right[...]))
            at += right.shape[1]


def middle_back(
    total_heads, scalars, total_ref, other_ref, middle_ref, cot_ref, gain_ref, sums_ref, gated_ref,
    gate_gain_ref, w_ref,
    dmiddle_ref, dmix_ref, dgain_ref, dnormed_ref, dattn_ref, cross_ref, dgate_gain_ref, full_ref,
):
    parity = scalars[scalars.shape[0] - 2]
    halves_joined(parity, total_ref, other_ref, full_ref)
    grad = full_ref[...]
    middle = middle_ref[...]
    inv = lax.rsqrt(jnp.mean(middle * middle, axis=-1, keepdims=True) + EPSILON)
    rows = middle * inv
    dgain_ref[...] = jnp.broadcast_to(jnp.sum(grad * rows, axis=0, keepdims=True), dgain_ref.shape)
    scaled = grad * gain_ref[...]
    dmiddle = cot_ref[...].astype(F32) + inv * (
        scaled - rows * jnp.mean(scaled * rows, axis=-1, keepdims=True)
    )
    dmiddle_ref[...] = dmiddle
    dmix_ref[...] = low(dmiddle)
    width = gated_ref.shape[1]
    first = w_ref.shape[1] - width - dattn_ref.shape[1]
    both = mm(dmix_ref[...], w_ref[:, first:])
    dnormed = both[:, :width]
    dnormed_ref[...] = dnormed
    dattn_ref[...] = low(both[:, width:])
    gated = gated_ref[...]
    product = dnormed * gated
    cross_ref[...] = token_sums(product * gate_gain_ref[...])
    inv_gate = as_column(lax.rsqrt(sums_ref[...] / (total_heads * PM) + EPSILON))
    dgate_gain_ref[...] = jnp.broadcast_to(
        jnp.sum(product * inv_gate, axis=0, keepdims=True), dgate_gain_ref.shape
    )


def gate_back(
    heads, total_heads, count, cross_ref, sums_ref, dnormed_ref, gated_ref, gain_ref, zq_ref, y_ref, cum_ref,
    bc_ref, *refs,
):
    msgs, kv = refs[: count - 1], refs[count - 1 : 2 * count - 1]
    dy_ref, dz_ref = refs[2 * count - 1 : 2 * count + 1]
    sent = refs[2 * count + 1 :]
    width = y_ref.shape[1]
    size = total_heads * PM
    inv = as_column(lax.rsqrt(sums_ref[...] / size + EPSILON))
    cross = as_column(cross_ref[...])
    dgated = inv * dnormed_ref[...] * gain_ref[...] - gated_ref[...] * (inv * inv * inv * cross / size)
    z = zq_ref[:, :width].astype(F32)
    sig = sigmoid(z)
    dy = dgated * (z * sig)
    dy_ref[...] = dy
    dz_ref[...] = low(dgated * y_ref[...] * sig * (1.0 + z * (1.0 - sig)))
    weighted = dy * mm(jnp.exp(cum_ref[...]), head_lanes(heads), HIGHEST)
    state = mm_tn(low(bc_ref[:, NS:]), low(weighted))
    for j in range(count):
        sent[j][:NS, :] = low(state)
        sent[j][NS:, :] = kv[j][...]
        if j < count - 1:
            decay = msgs[j][NS : NS + HALO, :].astype(F32)
            state = state * (decay[0:1, :] + decay[1:2, :])


def conv_and_input_back(
    scalars, dpre_ref, next_ref, taps_ref, dkv_ref, ddt_ref, dzq_ref,
    hidden_ref, dgain_mid_ref, dtaps_ref, dgate_gain_ref, dsmall_ref, dskip_ref, tokens_ref, w_ref, more_ref,
    dall_ref, small_ref, keep_ref, give_ref, full_ref,
):
    parity = scalars[scalars.shape[0] - 2]
    dpre = dpre_ref[...]
    rows = dpre.shape[0]
    longer = jnp.concatenate([dpre, next_ref[...]], axis=0)
    total = taps_ref[KC - 1 : KC, :] * dpre
    for k in range(KC - 1):
        shift = KC - 1 - k
        total = total + taps_ref[k : k + 1, :] * pltpu.roll(longer, longer.shape[0] - shift, 0)[:rows]
    dall = jnp.concatenate([low(total), dkv_ref[...], ddt_ref[...]], axis=1)
    dall_ref[...] = dall
    dzq = dzq_ref[...]
    full_ref[...] = mm_nt(dall, w_ref[...]) + mm_nt(dzq, more_ref[:, : dzq.shape[1]])
    x = tokens_ref[...].astype(F32)
    inv = lax.rsqrt(jnp.mean(x * x, axis=-1, keepdims=True) + EPSILON)
    dgain = jnp.sum(full_ref[...] * (x * inv), axis=0, keepdims=True)
    model = x.shape[1]
    place = lax.broadcasted_iota(jnp.int32, (8, model), 0)
    ddt_w = mm_tn(ddt_ref[...], hidden_ref[...])[:8]
    small_ref[:, :model] = jnp.where(place == 6, dgain_mid_ref[...], jnp.where(place == 7, dgain, ddt_w))
    rest = jnp.concatenate([dgate_gain_ref[0:1, :], dsmall_ref[0:1, :], dsmall_ref[1:2, :]], axis=1)
    wide = taps_ref.shape[1]
    skip_row = jnp.concatenate([dskip_ref[0:1, :], jnp.zeros((1, wide - LANES), F32)], axis=1)
    place = lax.broadcasted_iota(jnp.int32, (8, wide), 0)
    small_ref[:, model:] = jnp.where(
        place < KC, dtaps_ref[...], jnp.where(place == KC, rest, jnp.where(place == KC + 1, skip_row, 0.0))
    )
    halves_to_sum(parity, full_ref, keep_ref, give_ref)


def input_back(scalars, total_ref, other_ref, tokens_ref, gain_ref, dmiddle_ref, dtokens_ref, full_ref):
    parity = scalars[scalars.shape[0] - 2]
    halves_joined(parity, total_ref, other_ref, full_ref)
    grad = full_ref[...]
    x = tokens_ref[...].astype(F32)
    inv = lax.rsqrt(jnp.mean(x * x, axis=-1, keepdims=True) + EPSILON)
    rows = x * inv
    scaled = grad * gain_ref[...]
    dtokens_ref[...] = dmiddle_ref[...] + inv * (
        scaled - rows * jnp.mean(scaled * rows, axis=-1, keepdims=True)
    )


def output_sum(scalars, total_ref, other_ref, middle_ref, out_ref, full_ref):
    halves_joined(scalars[scalars.shape[0] - 2], total_ref, other_ref, full_ref)
    out_ref[...] = low(middle_ref[...] + full_ref[...])


def send(x, axis, pairs):
    return lax.ppermute(x, axis, pairs)


def from_ahead(x, axis, distance):
    n = lax.axis_size(axis)
    return send(x, axis, [((i + distance) % n, i) for i in range(n)])


def from_earlier(x, distance):
    n = lax.axis_size("row")
    return send(x, "row", [(i - distance, i) for i in range(distance, n)])


def from_later(x, distance):
    n = lax.axis_size("row")
    return send(x, "row", [(i + distance, i) for i in range(n - distance)])


def swap(x, axis, bit):
    return send(x, axis, [(i, i ^ bit) for i in range(lax.axis_size(axis))])


def after(x, *others):
    return lax.optimization_barrier((x,) + others)[0]


def after_all(*values):
    return lax.optimization_barrier(values)


def direct():
    return lax.axis_size("dp") == 2 and lax.axis_size("row") == 4


def scatter_first(parts):
    if len(parts) == 1:
        return [lax.psum_scatter(parts[0], ("dp", "row"), scatter_dimension=0, tiled=True)]
    half = parts[1].shape[0] // 2
    return [swap(parts[1][half:], "dp", 1), swap(parts[1][:half], "dp", 1)]


def scatter_beside(parts, got):
    if len(parts) == 1:
        return got[0]
    half = parts[0].shape[0] // 2
    return swap(low(parts[0][half:].astype(F32) + got[0].astype(F32)), "row", 1)


def scatter_last(parts, got, beside):
    if len(parts) == 1:
        return beside.astype(F32)
    blk = parts[0].shape[0] // 4
    total = parts[0][: 2 * blk].astype(F32) + got[1].astype(F32) + beside.astype(F32)
    return total[:blk] + swap(low(total[blk:]), "row", 2).astype(F32)


def col_sum(keep, give, *others):
    part = low(keep + swap(give, "col", 1).astype(F32))
    if others:
        part = after(part, *others)
    total = low(part.astype(F32) + swap(part, "col", 2).astype(F32))
    return total, swap(total, "col", 1)


def low_col_sum(values):
    values = low(values)
    values = low(values.astype(F32) + swap(values, "col", 1).astype(F32))
    return values.astype(F32) + swap(values, "col", 2).astype(F32)


def tiny_col_sum(values):
    values = values + swap(values, "col", 1)
    return values + swap(values, "col", 2)


def tiny_row_sum(values):
    if lax.axis_size("dp") == 2:
        values = values + swap(values, "dp", 1)
    else:
        values = lax.psum(values, "dp")
    values = values + swap(values, "row", 1)
    return values + swap(values, "row", 2)


def per_device(
    tokens, cotangent, norm_in, z_weight, x_weight, dt_weight, q_weight, bc_weight, key_value_weight,
    conv_x, conv_bc, dt_bias, a_log, d_skip, gate_gain, mamba_weight, attn_weight, norm_mid,
    gate_weight, up_weight, down_weight,
):
    dp_n, row_n, col_n = (lax.axis_size(a) for a in ("dp", "row", "col"))
    dp, row, col = (lax.axis_index(a) for a in ("dp", "row", "col"))
    if row_n != 4 or col_n != 4:
        raise ValueError("row, col: 4")
    rows, model = tokens.shape
    seq = rows * row_n
    heads = dt_bias.shape[0]
    total_heads = heads * col_n
    width = heads * PM
    q_width = q_weight.shape[1]
    q_heads = q_width // HEAD_DIM
    hidden = gate_weight.shape[1]
    blk = model // (dp_n * row_n)
    kv_group = col * q_heads * KEY_HEADS // QUERY_HEADS
    conv_width = width + 2 * NS
    in_width = conv_width + 2 * LANES

    shard_in = jnp.concatenate(
        [
            x_weight,
            bc_weight,
            lax.dynamic_slice_in_dim(key_value_weight, kv_group * HEAD_DIM, HEAD_DIM, 1),
            lax.dynamic_slice_in_dim(key_value_weight, (KEY_HEADS + kv_group) * HEAD_DIM, HEAD_DIM, 1),
            dt_weight,
            jnp.zeros((blk, LANES - heads), BF16),
        ],
        axis=1,
    )
    shard_mix = jnp.concatenate([z_weight, q_weight, mamba_weight.T, attn_weight.T], axis=1)
    shard_ff = jnp.concatenate([gate_weight, up_weight, down_weight.T], axis=1)
    halo = from_earlier(tokens[rows - HALO :], 1)
    ext = jnp.concatenate([halo, tokens], axis=0).astype(F32)
    inv_in = lax.rsqrt(jnp.mean(ext * ext, axis=-1, keepdims=True) + EPSILON)
    hidden_ext = low(ext * inv_in * norm_in)
    hidden_in = hidden_ext[HALO:]

    if direct():
        order = [((dp + i) % 2) * row_n + (row ^ x) for i in range(2) for x in (0, 2, 1, 3)]
        across, beside = swap(shard_in, "row", 2), swap(shard_in, "row", 1)
        own, mix_own = swap(shard_in, "dp", 1), swap(shard_mix, "dp", 1)
        across, beside, own, mix_own, hidden_ext = after_all(across, beside, own, mix_own, hidden_ext)
        corner = swap(across, "row", 1)
        over = [swap(across, "dp", 1), swap(beside, "dp", 1)]
        corner, shard_mix, shard_ff, *over = after_all(corner, shard_mix, shard_ff, *over)
        last = swap(corner, "dp", 1)
        mix_across, mix_beside = swap(shard_mix, "row", 2), swap(shard_mix, "row", 1)
        ff_own = swap(shard_ff, "dp", 1)
        last, mix_across, mix_beside, ff_own = after_all(last, mix_across, mix_beside, ff_own)
        in_blocks = [shard_in, across, beside, corner, own] + over + [last]
        mix_corner = swap(mix_across, "row", 1)
    else:
        in_blocks = [lax.all_gather(shard_in, ("dp", "row"), axis=0, tiled=True)]
        mix_blocks = [lax.all_gather(shard_mix, ("dp", "row"), axis=0, tiled=True)]
        ff_blocks = [lax.all_gather(shard_ff, ("dp", "row"), axis=0, tiled=True)]
        order = [jnp.int32(0)]
    scalars = jnp.stack([jnp.int32(v) for v in order] + [jnp.int32(col % 2), jnp.int32(row)])

    positions = (row * rows + jnp.arange(rows, dtype=jnp.int32)).astype(F32)
    half = HEAD_DIM // 2
    frequency = ROPE_BASE ** (-jnp.arange(half).astype(F32) / half)
    angles = positions[:, None] * frequency[None, :]
    cosine, sine = jnp.cos(angles), jnp.sin(angles)
    cos_q = jnp.concatenate([cosine] * (2 * q_heads), axis=1)
    sin_q = jnp.concatenate([sine] * (2 * q_heads), axis=1)
    cos_kv = jnp.concatenate([cosine, cosine, jnp.ones((rows, HEAD_DIM), F32)], axis=1)
    sin_kv = jnp.concatenate([sine, sine, jnp.zeros((rows, HEAD_DIM), F32)], axis=1)

    taps = jnp.concatenate([conv_x, conv_bc], axis=1)
    rate = -jnp.exp(a_log)

    def lane_row(v):
        return jnp.pad(v, (0, LANES - heads))[None, :]

    params = jnp.concatenate([lane_row(dt_bias), lane_row(rate), jnp.zeros((6, LANES), F32)], axis=0)
    skip = jnp.repeat(d_skip, PM)[None, :]
    area = rows * rows * heads
    part = packed_rows(rows, width)
    y_base, msg, proj, x_heads, bc_map, slope, cum, step, in_full = kernel_call(
        partial(scan_local, heads),
        (
            ((rows, width), F32),
            ((NS + HALO + 2 * part, width), BF16),
            ((HALO + rows, in_width), BF16),
            ((rows, width), F32),
            ((rows, 2 * NS), F32),
            ((rows, conv_width), F32),
            ((rows, LANES), F32),
            ((rows, LANES), F32),
        ),
        (area * 2 * PM * 10, 4000000, area),
        scalars,
        hidden_ext,
        taps,
        params,
        skip,
        cos_kv,
        sin_kv,
        in_blocks,
        keep=True,
    )
    if direct():
        msg, mix_corner, mix_across, mix_beside, shard_ff = after_all(
            msg, mix_corner, mix_across, mix_beside, shard_ff
        )
        msgs = [from_earlier(msg, j) for j in range(1, row_n)]
        mix_over = [swap(v, "dp", 1) for v in (mix_across, mix_beside, mix_corner)]
        ff_across, ff_beside = swap(shard_ff, "row", 2), swap(shard_ff, "row", 1)
        ff_across, ff_beside, *moved = after_all(ff_across, ff_beside, *mix_over, *msgs)
        mix_over, msgs = moved[:3], moved[3:]
        ff_corner = swap(ff_across, "row", 1)
        ff_over = [swap(v, "dp", 1) for v in (ff_across, ff_beside)]
        mix_blocks = [shard_mix, mix_across, mix_beside, mix_corner, mix_own] + mix_over
    else:
        msgs = [from_earlier(msg, j) for j in range(1, row_n)]
    zq, mix_full = kernel_call(
        project,
        (((rows, width + q_width), BF16),),
        (2 * rows * model * (width + q_width), 4000000, 0),
        scalars,
        hidden_in,
        mix_blocks,
        keep=True,
    )

    (
        attn_value, probs, query, key, value, state_in, carried, y, gated, sums,
    ) = kernel_call(
        partial(mix_tokens, heads, row_n - 1),
        (
            ((rows, q_width), BF16),
            ((q_heads * rows, seq), BF16),
            ((q_heads * rows, HEAD_DIM), BF16),
            ((seq, HEAD_DIM), BF16),
            ((seq, HEAD_DIM), BF16),
            ((NS, width), F32),
            ((rows, width), F32),
            ((rows, width), F32),
            ((rows, width), F32),
            ((8, rows), F32),
        ),
        (8 * q_width * rows * seq, 6000000, q_heads * rows * seq),
        scalars,
        msg,
        *msgs,
        y_base,
        cum,
        bc_map,
        zq,
        cos_q,
        sin_q,
    )
    sums = tiny_col_sum(sums)
    gain_row = gate_gain[None, :]
    halves = (((rows // 2, model), F32), ((rows // 2, model), BF16))
    full_scratch = ((rows, model), F32)
    mamba_normed, keep, give, _ = kernel_call(
        partial(mix_out, total_heads),
        (((rows, width), BF16),) + halves + (full_scratch,),
        (2 * rows * model * (width + q_width), 4000000, 0),
        scalars,
        sums,
        gated,
        gain_row,
        attn_value,
        mix_full,
    )
    if direct():
        give, ff_corner, *ff_over = after_all(give, ff_corner, *ff_over)
        ff_blocks = [shard_ff, ff_across, ff_beside, ff_corner, ff_own] + ff_over + [swap(ff_corner, "dp", 1)]
    total, other = col_sum(keep, give)

    gain_mid = norm_mid[None, :]
    middle, hidden_mid, grad_gate_up, swiglu, keep, give, out_keep, out_give, _ = kernel_call(
        feed_forward,
        (
            ((rows, model), F32),
            ((rows, model), BF16),
            ((rows, 2 * hidden), BF16),
            ((rows, hidden), BF16),
        )
        + halves
        + halves
        + (full_scratch,),
        (14 * rows * model * hidden, 8000000, rows * hidden),
        scalars,
        total,
        other,
        [tokens],
        [cotangent],
        gain_mid,
        ff_blocks,
    )

    def weight_grad(*operands):
        columns = sum(v.shape[1] for v in operands[1::2])
        outs = 2 if direct() else 1
        return kernel_call(
            partial(weight_products, len(order)),
            (((model // outs, columns), BF16),) * outs,
            (2 * rows * model * columns, 5000000, 0),
            scalars,
            *operands,
        )

    ff_parts = weight_grad(hidden_mid, grad_gate_up, cotangent, swiglu)
    total, other = col_sum(keep, give, *ff_parts)
    if direct():
        near = ff_parts[1].shape[0] // 2
        ff_got = [swap(ff_parts[1][near:], "dp", 1)]
    else:
        ff_got = scatter_first(ff_parts)

    grad_middle, grad_mix, dgain_mid, grad_normed, grad_attn, cross, dgate_gain, _ = kernel_call(
        partial(middle_back, total_heads),
        (
            ((rows, model), F32),
            ((rows, model), BF16),
            ((8, model), F32),
            ((rows, width), F32),
            ((rows, q_width), BF16),
            ((8, rows), F32),
            ((8, width), F32),
            full_scratch,
        ),
        (2 * rows * model * (width + q_width), 6000000, 0),
        scalars,
        total,
        other,
        middle,
        [cotangent],
        gain_mid,
        sums,
        gated,
        gain_row,
        mix_full,
    )
    cross = tiny_col_sum(cross)
    grad_query, grad_kv_own, *kv_sent = kernel_call(
        attend_back,
        (((rows, q_width), BF16), ((rows, LANES), F32)) + (((2 * part, width), BF16),) * (row_n - 1),
        (16 * q_width * rows * seq, 4000000, 0),
        None,
        grad_attn,
        probs,
        query,
        cos_q,
        sin_q,
        key,
        value,
    )
    grad_y, grad_z, *sent = kernel_call(
        partial(gate_back, heads, total_heads, row_n - 1),
        (((rows, width), F32), ((rows, width), BF16)) + (((NS + 2 * part, width), BF16),) * (row_n - 1),
        (2 * rows * NS * width, 4000000, rows * width),
        None,
        cross,
        sums,
        grad_normed,
        gated,
        gain_row,
        zq,
        y,
        cum,
        bc_map,
        *msgs[: row_n - 2],
        *kv_sent,
    )
    got = [from_later(sent[j - 1], j) for j in range(1, row_n)]
    if direct():
        ff_got.append(swap(after(ff_parts[1][:near], grad_y), "dp", 1))
    dx_local, dbc_local, dcum, dstep, dskip = kernel_call(
        partial(scan_back_local, heads),
        (
            ((rows, width), F32),
            ((rows, 2 * NS), F32),
            ((rows, LANES), F32),
            ((rows, LANES), F32),
            ((8, LANES), F32),
        ),
        (area * 2 * PM * 20, 4000000, area),
        None,
        grad_y,
        x_heads,
        bc_map,
        cum,
        step,
        carried,
        state_in,
        skip,
    )
    grad_zq = jnp.concatenate([grad_z, grad_query], axis=1)
    act = jnp.concatenate([mamba_normed, attn_value], axis=1)
    mix_parts = weight_grad(hidden_in, grad_zq, grad_mix, act)
    mix_got = scatter_first(mix_parts)
    got = list(after(tuple(got), mix_parts, ff_got[0]))

    dpre, first, grad_dt, grad_kv, dsmall, dtaps = kernel_call(
        partial(scan_back_end, heads, row_n - 1),
        (
            ((rows, conv_width), F32),
            ((8, conv_width), F32),
            ((rows, LANES), BF16),
            ((rows, LANES), BF16),
            ((8, LANES), F32),
            ((8, conv_width), F32),
        ),
        (rows * NS * width * 10, 4000000, rows * LANES * 3),
        None,
        *got,
        state_in,
        x_heads,
        bc_map,
        cum,
        step,
        dx_local,
        dbc_local,
        dcum,
        dstep,
        slope,
        proj,
        params,
        grad_kv_own,
        cos_kv,
        sin_kv,
    )
    following = from_later(first, 1)
    following = after(following, ff_got)
    ff_beside = scatter_beside(ff_parts, [after(ff_got[0], following)])

    grad_all, small, keep, give, _ = kernel_call(
        conv_and_input_back,
        (((rows, in_width), BF16), ((8, model + conv_width), F32)) + halves + (full_scratch,),
        (2 * rows * model * (in_width + width + q_width), 8000000, 0),
        scalars,
        dpre,
        following,
        taps,
        grad_kv,
        grad_dt,
        grad_zq,
        hidden_in,
        dgain_mid,
        dtaps,
        dgate_gain,
        dsmall,
        dskip,
        [tokens],
        in_full,
        mix_full,
    )
    tail_width = conv_width + LANES
    tail_parts = weight_grad(hidden_in, after(grad_all, mix_got[0])[:, :tail_width])
    mix_got = mix_got[:1] + [after(v, *tail_parts) for v in mix_got[1:]]
    tail_got = scatter_first(tail_parts)
    mix_beside = scatter_beside(mix_parts, [after(mix_got[0], ff_beside, tail_got)])
    total, other = col_sum(keep, give)
    grad_ff = scatter_last(ff_parts, ff_got, after(ff_beside, tail_got[0]))
    out_total, out_other = col_sum(out_keep, after(out_give, total))
    layer_out, _ = kernel_call(
        output_sum,
        (((rows, model), BF16), full_scratch),
        (rows * model, 3000000, 0),
        scalars,
        out_total,
        out_other,
        middle,
    )
    tail_beside = scatter_beside(tail_parts, [after(tail_got[0], ff_beside)])
    grad_in_w = scatter_last(tail_parts, tail_got, tail_beside)
    grad_mix_w = scatter_last(mix_parts, mix_got, after(mix_beside, tail_beside))
    grad_tokens, _ = kernel_call(
        input_back,
        (((rows, model), F32), full_scratch),
        (rows * model * 10, 4000000, 0),
        scalars,
        total,
        other,
        [tokens],
        norm_in[None, :],
        [grad_middle],
    )

    bc_w = grad_in_w[:, width:conv_width]
    kv_w = grad_in_w[:, conv_width:]
    spot = (jnp.arange(KEY_HEADS) == kv_group).astype(F32)
    wide = [spot[i] * kv_w[:, :HEAD_DIM] for i in range(KEY_HEADS)]
    wide += [spot[i] * kv_w[:, HEAD_DIM:] for i in range(KEY_HEADS)]
    shared = jnp.concatenate([bc_w] + wide, axis=1)
    shared = low_col_sum(shared)

    line = lax.broadcasted_iota(jnp.int32, small.shape, 0)
    lane = lax.broadcasted_iota(jnp.int32, small.shape, 1)
    partial_lanes = ((line == 7) & (lane < model)) | ((line < KC) & (lane >= model + width))
    small = jnp.where(partial_lanes, tiny_col_sum(small), small)
    small = tiny_row_sum(after(small, tail_beside))
    taps_at = model + width
    place = (dp * row_n + row) * blk
    return (
        layer_out,
        grad_tokens,
        small[7, :model],
        grad_mix_w[:, :width],
        grad_in_w[:, :width],
        lax.dynamic_slice(small, (0, place), (heads, blk)).T,
        grad_mix_w[:, width : width + q_width],
        shared[:, : 2 * NS],
        shared[:, 2 * NS :],
        small[:KC, model:taps_at],
        small[:KC, taps_at:],
        small[KC, taps_at : taps_at + heads],
        small[KC, taps_at + LANES : taps_at + LANES + heads],
        small[KC + 1, model : model + heads],
        small[KC, model:taps_at],
        grad_mix_w[:, width + q_width : 2 * width + q_width].T,
        grad_mix_w[:, 2 * width + q_width :].T,
        small[6, :model],
        grad_ff[:, :hidden],
        grad_ff[:, hidden : 2 * hidden],
        grad_ff[:, 2 * hidden :].T,
    )


def solution(mesh):
    by_rows = P(("dp", "row"), None)
    both = P(("dp", "row"), "col")
    turned = P("col", ("dp", "row"))
    per_col = P("col")
    taps = P(None, "col")
    in_specs = (
        by_rows, by_rows, P(), both, both, both, both, by_rows, by_rows, taps, P(), per_col, per_col,
        per_col, per_col, turned, turned, P(), both, both, turned,
    )
    out_specs = (
        by_rows, by_rows, P(), both, both, both, both, by_rows, by_rows, taps, P(), per_col, per_col,
        per_col, per_col, turned, turned, P(), both, both, turned,
    )
    return jax.shard_map(
        per_device, mesh=mesh, in_specs=in_specs, out_specs=out_specs, check_vma=False
    )
```

profile of v0, /device:TPU:0, one launch (start us, length us, event | category | flops | bytes accessed | tf_op | source)
XLA Modules:
  0.0 284.9 jit_solution(7657307994171122089)
XLA Ops:
  3.6 4.1 %collective-permute-start = (bf16[128,896]{1,0:T(8,128)(2,1)S(1)}, bf16[128,896]{1,0:T(8,128)(2,1)S(1)}, u32[]{:S(2)}, u32[]{:S(2)}) collective-permute-start(bf16[128,896]{1,0:T(8,128)(2,1)S(1)} %concatenate.40.refs_7_), channel_id=1, source_target_pairs={{0,8},{4,12},{8,0},{12,4},{1,9},{5,13},{9,1},{13,5},{2,10},{6,14},... | collective-permute-start | bytes 688136 | tf_op jit(solution)/shard_map/ppermute | solution.py:618
  18.7 5.1 %collective-permute-done.3.refs_6_ = bf16[128,1024]{1,0:T(8,128)(2,1)S(1)} collective-permute-done((bf16[128,1024]{1,0:T(8,128)(2,1)S(1)}, bf16[128,1024]{1,0:T(8,128)(2,1)S(1)}, u32[]{:S(2)}, u32[]{:S(2)}) %collective-permute-start.3) | collective-permute-done | bytes 262176 | tf_op jit(solution)/shard_map/ppermute | solution.py:618
  41.0 6.6 %collective-permute-done.8.refs_14_ = bf16[128,896]{1,0:T(8,128)(2,1)S(1)} collective-permute-done((bf16[128,896]{1,0:T(8,128)(2,1)}, bf16[128,896]{1,0:T(8,128)(2,1)S(1)}, u32[]{:S(2)}, u32[]{:S(2)}) %collective-permute-start.8) | collective-permute-done | bytes 229408 | tf_op jit(solution)/shard_map/ppermute | solution.py:618
  53.0 6.1 %shard_map.364 = (f32[256,384]{1,0:T(8,128)S(1)}, bf16[240,384]{1,0:T(8,128)(2,1)S(1)}, bf16[272,896]{1,0:T(8,128)(2,1)S(1)}, f32[256,384]{1,0:T(8,128)S(1)}, f3...) custom-call(s32[10]{0:T(128)S(1)} %stack.43.refs_0_, ...), custom_call_target="tpu_custom_call" | custom-call | flops 503316480 | bytes 4000000 | tf_op jit(solution)/shard_map/pallas_call | solution.py:120
  59.8 3.7 %collective-permute-start.18 = (bf16[240,384]{1,0:T(8,128)(2,1)S(1)}, bf16[240,384]{1,0:T(8,128)(2,1)S(1)}, u32[]{:S(2)}, u32[]{:S(2)}) collective-permute-start(bf16[240,384]{1,0:T(8,128)(2,1)S(1)} %get-tuple-element.152.refs_1_), channel_id=1, source_target_pairs={{0,4},{4,8},{8,12},{1,5},{5,9},{9,13},{2,6},{6,10},{10,14},{3,7},{... | collective-permute-start | bytes 552968 | tf_op jit(solution)/shard_map/ppermute | solution.py:618
  69.3 3.2 %collective-permute-done.19.refs_3_.refs_10_ = bf16[240,384]{1,0:T(8,128)(2,1)S(1)} collective-permute-done((bf16[240,384]{1,0:T(8,128)(2,1)S(1)}, bf16[240,384]{1,0:T(8,128)(2,1)S(1)}, u32[]{:S(2)}, u32[]{:S(2)}) %collective-permute-start.19) | collective-permute-done | bytes 184352 | tf_op jit(solution)/shard_map/ppermute | solution.py:618
  73.3 3.2 %collective-permute-done.20.refs_4_ = bf16[240,384]{1,0:T(8,128)(2,1)S(1)} collective-permute-done((bf16[240,384]{1,0:T(8,128)(2,1)S(1)}, bf16[240,384]{1,0:T(8,128)(2,1)S(1)}, u32[]{:S(2)}, u32[]{:S(2)}) %collective-permute-start.20) | collective-permute-done | bytes 184352 | tf_op jit(solution)/shard_map/ppermute | solution.py:618
  77.8 4.7 %collective-permute-done.16.refs_8_ = bf16[128,1024]{1,0:T(8,128)(2,1)S(1)} collective-permute-done((bf16[128,1024]{1,0:T(8,128)(2,1)S(1)}, bf16[128,1024]{1,0:T(8,128)(2,1)S(1)}, u32[]{:S(2)}, u32[]{:S(2)}) %collective-permute-start.16) | collective-permute-done | bytes 262176 | tf_op jit(solution)/shard_map/ppermute | solution.py:618
  85.3 5.9 %collective-permute-done.14.refs_8_ = bf16[128,1536]{1,0:T(8,128)(2,1)S(1)} collective-permute-done((bf16[128,1536]{1,0:T(8,128)(2,1)S(1)}, bf16[128,1536]{1,0:T(8,128)(2,1)S(1)}, u32[]{:S(2)}, u32[]{:S(2)}) %collective-permute-start.14) | collective-permute-done | bytes 393248 | tf_op jit(solution)/shard_map/ppermute | solution.py:618
  91.2 11.4 %collective-permute-start.23 = (bf16[128,1536]{1,0:T(8,128)(2,1)S(1)}, bf16[128,1536]{1,0:T(8,128)(2,1)S(1)}, u32[]{:S(2)}, u32[]{:S(2)}) collective-permute-start(bf16[128,1536]{1,0:T(8,128)(2,1)S(1)} %collective-permute-done.13.refs_7_), channel_id=1, source_target_pairs={{0,4},{4,0},{8,12},{12,8},{1,5},{5,1},{9,13},{13,9},{2,6},{6,2},{1... | collective-permute-start | bytes 1179656 | tf_op jit(solution)/shard_map/ppermute | solution.py:618
  107.9 3.3 %shard_map.366 = (bf16[256,128]{1,0:T(8,128)(2,1)S(1)}, bf16[512,1024]{1,0:T(8,128)(2,1)S(1)}, bf16[512,64]{1,0:T(8,128)(2,1)S(1)}, bf16[1024,64]{1,0:T(8,128)(2...) custom-call(s32[10]{0:T(128)S(1)} %stack.43.refs_0_, ...), custom_call_target="tpu_custom_call" | custom-call | flops 268435456 | bytes 6000000 | tf_op jit(solution)/shard_map/pallas_call | solution.py:120
  122.9 6.8 %collective-permute-done.27 = bf16[128,1024]{1,0:T(8,128)(2,1)S(1)} collective-permute-done((bf16[128,1024]{1,0:T(8,128)(2,1)S(1)}, bf16[128,1024]{1,0:T(8,128)(2,1)S(1)}, u32[]{:S(2)}, u32[]{:S(2)}) %collective-permute-start.27) | collective-permute-done | bytes 262176 | tf_op jit(solution)/shard_map/ppermute | solution.py:618
  129.9 3.8 %collective-permute-done.29.refs_13_ = bf16[128,1536]{1,0:T(8,128)(2,1)S(1)} collective-permute-done((bf16[128,1536]{1,0:T(8,128)(2,1)S(1)}, bf16[128,1536]{1,0:T(8,128)(2,1)S(1)}, u32[]{:S(2)}, u32[]{:S(2)}) %collective-permute-start.29) | collective-permute-done | bytes 393248 | tf_op jit(solution)/shard_map/ppermute | solution.py:618
  133.8 5.7 %shard_map.368 = (f32[256,1024]{1,0:T(8,128)S(1)}, bf16[256,1024]{1,0:T(8,128)(2,1)S(1)}, bf16[256,1024]{1,0:T(8,128)(2,1)S(1)}, bf16[256,512]{1,0:T(8,128)(2,1)...) custom-call(s32[10]{0:T(128)S(1)} %stack.43.refs_0_, ...), custom_call_target="tpu_custom_call" | custom-call | flops 1879048192 | bytes 8000000 | tf_op jit(solution)/shard_map/pallas_call | solution.py:120
  142.5 7.5 %collective-permute-done.31 = bf16[128,1024]{1,0:T(8,128)(2,1)S(1)} collective-permute-done((bf16[128,1024]{1,0:T(8,128)(2,1)S(1)}, bf16[128,1024]{1,0:T(8,128)(2,1)S(1)}, u32[]{:S(2)}, u32[]{:S(2)}) %collective-permute-start.31) | collective-permute-done | bytes 262176 | tf_op jit(solution)/shard_map/ppermute | solution.py:618
  151.8 3.0 %shard_map.370 = (f32[256,1024]{1,0:T(8,128)S(1)}, bf16[256,1024]{1,0:T(8,128)(2,1)S(1)}, f32[8,1024]{1,0:T(8,128)S(1)}, f32[256,384]{1,0:T(8,128)S(1)}, bf16[25...) custom-call(s32[10]{0:T(128)S(1)} %stack.43.refs_0_, ...), custom_call_target="tpu_custom_call" | custom-call | flops 268435456 | bytes 6000000 | tf_op jit(solution)/shard_map/pallas_call | solution.py:120
  178.7 8.4 %collective-permute-done.36.refs_1_ = bf16[224,384]{1,0:T(8,128)(2,1)S(1)} collective-permute-done((bf16[224,384]{1,0:T(8,128)(2,1)}, bf16[224,384]{1,0:T(8,128)(2,1)S(1)}, u32[]{:S(2)}, u32[]{:S(2)}) %collective-permute-start.36) | collective-permute-done | bytes 172064 | tf_op jit(solution)/shard_map/ppermute | solution.py:618
  200.0 5.9 %collective-permute-done.49 = bf16[256,1024]{1,0:T(8,128)(2,1)S(1)} collective-permute-done((bf16[256,1024]{1,0:T(8,128)(2,1)S(1)}, bf16[256,1024]{1,0:T(8,128)(2,1)S(1)}, u32[]{:S(2)}, u32[]{:S(2)}) %collective-permute-start.49) | collective-permute-done | bytes 524320 | tf_op jit(solution)/shard_map/ppermute | solution.py:618
  208.4 8.7 %collective-permute-done.56 = bf16[256,1024]{1,0:T(8,128)(2,1)S(1)} collective-permute-done((bf16[256,1024]{1,0:T(8,128)(2,1)S(1)}, bf16[256,1024]{1,0:T(8,128)(2,1)S(1)}, u32[]{:S(2)}, u32[]{:S(2)}) %collective-permute-start.56) | collective-permute-done | bytes 524320 | tf_op jit(solution)/shard_map/ppermute | solution.py:618
  221.9 3.5 %collective-permute-done.42 = bf16[128,1024]{1,0:T(8,128)(2,1)S(1)} collective-permute-done((bf16[128,1024]{1,0:T(8,128)(2,1)S(1)}, bf16[128,1024]{1,0:T(8,128)(2,1)S(1)}, u32[]{:S(2)}, u32[]{:S(2)}) %collective-permute-start.42) | collective-permute-done | bytes 262176 | tf_op jit(solution)/shard_map/ppermute | solution.py:618
  239.1 6.7 %collective-permute-done.52 = bf16[256,768]{1,0:T(8,128)(2,1)S(1)} collective-permute-done((bf16[256,768]{1,0:T(8,128)(2,1)S(1)}, bf16[256,768]{1,0:T(8,128)(2,1)S(1)}, u32[]{:S(2)}, u32[]{:S(2)}) %collective-permute-start.52) | collective-permute-done | bytes 393248 | tf_op jit(solution)/shard_map/ppermute | solution.py:618
  254.2 5.4 %collective-permute-start.60 = (bf16[128,768]{1,0:T(8,128)(2,1)S(1)}, bf16[128,768]{1,0:T(8,128)(2,1)S(1)}, u32[]{:S(2)}, u32[]{:S(2)}) collective-permute-start(bf16[128,768]{1,0:T(8,128)(2,1)S(1)} %slice.241), channel_id=1, source_target_pairs={{0,8},{4,12},{8,0},{12,4},{1,9},{5,13},{9,1},{13,5},{2,10},{6,14},... | collective-permute-start | bytes 589832 | tf_op jit(solution)/shard_map/ppermute | solution.py:618
  259.6 4.2 %collective-permute-done.54 = f32[8,1664]{1,0:T(8,128)S(1)} collective-permute-done((f32[8,1664]{1,0:T(8,128)S(1)}, f32[8,1664]{1,0:T(8,128)S(1)}, u32[]{:S(2)}, u32[]{:S(2)}) %collective-permute-start.54) | collective-permute-done | bytes 53280 | tf_op jit(solution)/shard_map/ppermute | solution.py:618
  277.0 4.2 %collective-permute-done.59 = bf16[128,1024]{1,0:T(8,128)(2,1)S(1)} collective-permute-done((bf16[128,1024]{1,0:T(8,128)(2,1)S(1)}, bf16[128,1024]{1,0:T(8,128)(2,1)S(1)}, u32[]{:S(2)}, u32[]{:S(2)}) %collective-permute-start.59) | collective-permute-done | bytes 262176 | tf_op jit(solution)/shard_map/ppermute | solution.py:618
  (388 shorter events, 151.6 us)
Async XLA Ops:
  3.6 15.1 %collective-permute-start = (bf16[128,896]{1,0:T(8,128)(2,1)S(1)}, bf16[128,896]{1,0:T(8,128)(2,1)S(1)}, u32[]{:S(2)}, u32[]{:S(2)}) collective-permute-start(bf16[128,896]{1,0:T(8,128)(2,1)S(1)} %concatenate.40.refs_7_), channel_id=1, source_target_pairs={{0,8},{4,12},{8,0},{12,4},{1,9},{5,13},{9,1},{13,5},{2,10},{6,14},... | collective-permute-start | bytes 688136 | tf_op jit(solution)/shard_map/ppermute | solution.py:618
  34.9 14.0 %collective-permute-start.11 = (bf16[128,1536]{1,0:T(8,128)(2,1)S(1)}, bf16[128,1536]{1,0:T(8,128)(2,1)}, u32[]{:S(2)}, u32[]{:S(2)}) collective-permute-start(bf16[128,1536]{1,0:T(8,128)(2,1)S(1)} %pad_maximum_fusion.1.refs_6_), channel_id=1, source_target_pairs={{0,16},{16,0},{1,17},{17,1},{2,18},{18,2},{3,19},{19,3},{4,20},{20... | collective-permute-start | bytes 1179656 | tf_op jit(solution)/shard_map/ppermute | solution.py:618
  67.4 17.9 %collective-permute-start.13 = (bf16[128,1536]{1,0:T(8,128)(2,1)S(1)}, bf16[128,1536]{1,0:T(8,128)(2,1)S(1)}, u32[]{:S(2)}, u32[]{:S(2)}) collective-permute-start(bf16[128,1536]{1,0:T(8,128)(2,1)S(1)} %pad_maximum_fusion.1.refs_6_), channel_id=1, source_target_pairs={{0,8},{4,12},{8,0},{12,4},{1,9},{5,13},{9,1},{13,5},{2,10},{6,14},... | collective-permute-start | bytes 1179656 | tf_op jit(solution)/shard_map/ppermute | solution.py:618
  67.5 23.8 %collective-permute-start.14 = (bf16[128,1536]{1,0:T(8,128)(2,1)S(1)}, bf16[128,1536]{1,0:T(8,128)(2,1)S(1)}, u32[]{:S(2)}, u32[]{:S(2)}) collective-permute-start(bf16[128,1536]{1,0:T(8,128)(2,1)S(1)} %pad_maximum_fusion.1.refs_6_), channel_id=1, source_target_pairs={{0,4},{4,0},{8,12},{12,8},{1,5},{5,1},{9,13},{13,9},{2,6},{6,2},{1... | collective-permute-start | bytes 1179656 | tf_op jit(solution)/shard_map/ppermute | solution.py:618
  91.2 28.4 %collective-permute-start.23 = (bf16[128,1536]{1,0:T(8,128)(2,1)S(1)}, bf16[128,1536]{1,0:T(8,128)(2,1)S(1)}, u32[]{:S(2)}, u32[]{:S(2)}) collective-permute-start(bf16[128,1536]{1,0:T(8,128)(2,1)S(1)} %collective-permute-done.13.refs_7_), channel_id=1, source_target_pairs={{0,4},{4,0},{8,12},{12,8},{1,5},{5,1},{9,13},{13,9},{2,6},{6,2},{1... | collective-permute-start | bytes 1179656 | tf_op jit(solution)/shard_map/ppermute | solution.py:618
  102.6 17.0 %collective-permute-start.24 = (bf16[128,1536]{1,0:T(8,128)(2,1)S(1)}, bf16[128,1536]{1,0:T(8,128)(2,1)S(1)}, u32[]{:S(2)}, u32[]{:S(2)}) collective-permute-start(bf16[128,1536]{1,0:T(8,128)(2,1)S(1)} %collective-permute-done.13.refs_7_), channel_id=1, source_target_pairs={{0,16},{16,0},{1,17},{17,1},{2,18},{18,2},{3,19},{19,3},{4,20},{20... | collective-permute-start | bytes 1179656 | tf_op jit(solution)/shard_map/ppermute | solution.py:618
  102.6 17.0 %collective-permute-start.25 = (bf16[128,1536]{1,0:T(8,128)(2,1)S(1)}, bf16[128,1536]{1,0:T(8,128)(2,1)S(1)}, u32[]{:S(2)}, u32[]{:S(2)}) collective-permute-start(bf16[128,1536]{1,0:T(8,128)(2,1)S(1)} %collective-permute-done.14.refs_8_), channel_id=1, source_target_pairs={{0,16},{16,0},{1,17},{17,1},{2,18},{18,2},{3,19},{19,3},{4,20},{20... | collective-permute-start | bytes 1179656 | tf_op jit(solution)/shard_map/ppermute | solution.py:618
  151.5 27.2 %collective-permute-start.38 = (bf16[256,1536]{1,0:T(8,128)(2,1)}, bf16[256,1536]{1,0:T(8,128)(2,1)}, u32[]{:S(2)}, u32[]{:S(2)}) collective-permute-start(bf16[256,1536]{1,0:T(8,128)(2,1)} %get-tuple-element.279), channel_id=1, source_target_pairs={{0,16},{16,0},{1,17},{17,1},{2,18},{18,2},{3,19},{19,3},{4,20},{20... | collective-permute-start | bytes 2359304 | tf_op jit(solution)/shard_map/ppermute | solution.py:618
  164.1 31.1 %collective-permute-start.40 = (bf16[256,1536]{1,0:T(8,128)(2,1)}, bf16[256,1536]{1,0:T(8,128)(2,1)}, u32[]{:S(2)}, u32[]{:S(2)}) collective-permute-start(bf16[256,1536]{1,0:T(8,128)(2,1)} %get-tuple-element.229), channel_id=1, source_target_pairs={{0,16},{16,0},{1,17},{17,1},{2,18},{18,2},{3,19},{19,3},{4,20},{20... | collective-permute-start | bytes 2359304 | tf_op jit(solution)/shard_map/ppermute | solution.py:618
  168.7 18.4 %collective-permute-start.36 = (bf16[224,384]{1,0:T(8,128)(2,1)}, bf16[224,384]{1,0:T(8,128)(2,1)S(1)}, u32[]{:S(2)}, u32[]{:S(2)}) collective-permute-start(bf16[224,384]{1,0:T(8,128)(2,1)} %copy-done.72), channel_id=1, source_target_pairs={{8,0},{12,4},{9,1},{13,5},{10,2},{14,6},{11,3},{15,7},{24,16},{28,... | collective-permute-start | bytes 516104 | tf_op jit(solution)/shard_map/ppermute | solution.py:618
  170.0 17.1 %collective-permute-start.37 = (bf16[224,384]{1,0:T(8,128)(2,1)}, bf16[224,384]{1,0:T(8,128)(2,1)S(1)}, u32[]{:S(2)}, u32[]{:S(2)}) collective-permute-start(bf16[224,384]{1,0:T(8,128)(2,1)} %copy-done.71), channel_id=1, source_target_pairs={{12,0},{13,1},{14,2},{15,3},{28,16},{29,17},{30,18},{31,19}} | collective-permute-start | bytes 516104 | tf_op jit(solution)/shard_map/ppermute | solution.py:618
  190.9 14.9 %collective-permute-start.49 = (bf16[256,1024]{1,0:T(8,128)(2,1)S(1)}, bf16[256,1024]{1,0:T(8,128)(2,1)S(1)}, u32[]{:S(2)}, u32[]{:S(2)}) collective-permute-start(bf16[256,1024]{1,0:T(8,128)(2,1)S(1)} %get-tuple-element.281), channel_id=1, source_target_pairs={{0,16},{16,0},{1,17},{17,1},{2,18},{18,2},{3,19},{19,3},{4,20},{20... | collective-permute-start | bytes 1572872 | tf_op jit(solution)/shard_map/ppermute | solution.py:618
  191.5 25.6 %collective-permute-start.56 = (bf16[256,1024]{1,0:T(8,128)(2,1)S(1)}, bf16[256,1024]{1,0:T(8,128)(2,1)S(1)}, u32[]{:S(2)}, u32[]{:S(2)}) collective-permute-start(bf16[256,1024]{1,0:T(8,128)(2,1)S(1)} %get-tuple-element.280), channel_id=1, source_target_pairs={{0,16},{16,0},{1,17},{17,1},{2,18},{18,2},{3,19},{19,3},{4,20},{20... | collective-permute-start | bytes 1572872 | tf_op jit(solution)/shard_map/ppermute | solution.py:618
  196.5 29.5 %collective-permute-start.51 = (bf16[256,1536]{1,0:T(8,128)(2,1)S(1)}, bf16[256,1536]{1,0:T(8,128)(2,1)S(1)}, u32[]{:S(2)}, u32[]{:S(2)}) collective-permute-start(bf16[256,1536]{1,0:T(8,128)(2,1)S(1)} %add_convert_fusion), channel_id=1, source_target_pairs={{0,4},{4,0},{8,12},{12,8},{1,5},{5,1},{9,13},{13,9},{2,6},{6,2},{1... | collective-permute-start | bytes 2359304 | tf_op jit(solution)/shard_map/ppermute | solution.py:618
  205.9 13.0 %collective-permute-start.41 = (bf16[128,1024]{1,0:T(8,128)(2,1)S(1)}, bf16[128,1024]{1,0:T(8,128)(2,1)S(1)}, u32[]{:S(2)}, u32[]{:S(2)}) collective-permute-start(bf16[128,1024]{1,0:T(8,128)(2,1)S(1)} %get-tuple-element.240), channel_id=1, source_target_pairs={{0,1},{1,0},{2,3},{3,2},{4,5},{5,4},{6,7},{7,6},{8,9},{9,8},{10,11... | collective-permute-start | bytes 786440 | tf_op jit(solution)/shard_map/ppermute | solution.py:618
  207.8 18.3 %collective-permute-start.50 = (bf16[256,768]{1,0:T(8,128)(2,1)S(1)}, bf16[256,768]{1,0:T(8,128)(2,1)S(1)}, u32[]{:S(2)}, u32[]{:S(2)}) collective-permute-start(bf16[256,768]{1,0:T(8,128)(2,1)S(1)} %get-tuple-element.286), channel_id=1, source_target_pairs={{0,16},{16,0},{1,17},{17,1},{2,18},{18,2},{3,19},{19,3},{4,20},{20... | collective-permute-start | bytes 1179656 | tf_op jit(solution)/shard_map/ppermute | solution.py:618
  217.1 14.4 %collective-permute-start.57 = (bf16[256,768]{1,0:T(8,128)(2,1)S(1)}, bf16[256,768]{1,0:T(8,128)(2,1)S(1)}, u32[]{:S(2)}, u32[]{:S(2)}) collective-permute-start(bf16[256,768]{1,0:T(8,128)(2,1)S(1)} %get-tuple-element.285), channel_id=1, source_target_pairs={{0,16},{16,0},{1,17},{17,1},{2,18},{18,2},{3,19},{19,3},{4,20},{20... | collective-permute-start | bytes 1179656 | tf_op jit(solution)/shard_map/ppermute | solution.py:618
  227.5 20.6 %collective-permute-start.63 = (bf16[128,1536]{1,0:T(8,128)(2,1)S(1)}, bf16[128,1536]{1,0:T(8,128)(2,1)S(1)}, u32[]{:S(2)}, u32[]{:S(2)}) collective-permute-start(bf16[128,1536]{1,0:T(8,128)(2,1)S(1)} %slice.239), channel_id=1, source_target_pairs={{0,8},{4,12},{8,0},{12,4},{1,9},{5,13},{9,1},{13,5},{2,10},{6,14},... | collective-permute-start | bytes 1179656 | tf_op jit(solution)/shard_map/ppermute | solution.py:618
  228.0 17.8 %collective-permute-start.52 = (bf16[256,768]{1,0:T(8,128)(2,1)S(1)}, bf16[256,768]{1,0:T(8,128)(2,1)S(1)}, u32[]{:S(2)}, u32[]{:S(2)}) collective-permute-start(bf16[256,768]{1,0:T(8,128)(2,1)S(1)} %add_convert_fusion.2), channel_id=1, source_target_pairs={{0,4},{4,0},{8,12},{12,8},{1,5},{5,1},{9,13},{13,9},{2,6},{6,2},{1... | collective-permute-start | bytes 1179656 | tf_op jit(solution)/shard_map/ppermute | solution.py:618
  234.3 31.3 %collective-permute-start.58 = (bf16[256,1024]{1,0:T(8,128)(2,1)}, bf16[256,1024]{1,0:T(8,128)(2,1)}, u32[]{:S(2)}, u32[]{:S(2)}) collective-permute-start(bf16[256,1024]{1,0:T(8,128)(2,1)} %add_convert_fusion.1), channel_id=1, source_target_pairs={{0,4},{4,0},{8,12},{12,8},{1,5},{5,1},{9,13},{13,9},{2,6},{6,2},{1... | collective-permute-start | bytes 1572872 | tf_op jit(solution)/shard_map/ppermute | solution.py:618
  239.0 29.5 %collective-permute-start.45 = (bf16[128,1024]{1,0:T(8,128)(2,1)S(1)}, bf16[128,1024]{1,0:T(8,128)(2,1)S(1)}, u32[]{:S(2)}, u32[]{:S(2)}) collective-permute-start(bf16[128,1024]{1,0:T(8,128)(2,1)S(1)} %add_convert_fusion.3.refs_1_), channel_id=1, source_target_pairs={{0,1},{1,0},{2,3},{3,2},{4,5},{5,4},{6,7},{7,6},{8,9},{9,8},{10,11... | collective-permute-start | bytes 786440 | tf_op jit(solution)/shard_map/ppermute | solution.py:618
  249.9 13.9 %collective-permute-start.54 = (f32[8,1664]{1,0:T(8,128)S(1)}, f32[8,1664]{1,0:T(8,128)S(1)}, u32[]{:S(2)}, u32[]{:S(2)}) collective-permute-start(f32[8,1664]{1,0:T(8,128)S(1)} %add.215), channel_id=1, source_target_pairs={{0,4},{4,0},{8,12},{12,8},{1,5},{5,1},{9,13},{13,9},{2,6},{6,2},{1... | collective-permute-start | bytes 159752 | tf_op jit(solution)/shard_map/ppermute | solution.py:618
  254.2 17.2 %collective-permute-start.60 = (bf16[128,768]{1,0:T(8,128)(2,1)S(1)}, bf16[128,768]{1,0:T(8,128)(2,1)S(1)}, u32[]{:S(2)}, u32[]{:S(2)}) collective-permute-start(bf16[128,768]{1,0:T(8,128)(2,1)S(1)} %slice.241), channel_id=1, source_target_pairs={{0,8},{4,12},{8,0},{12,4},{1,9},{5,13},{9,1},{13,5},{2,10},{6,14},... | collective-permute-start | bytes 589832 | tf_op jit(solution)/shard_map/ppermute | solution.py:618
  267.1 14.0 %collective-permute-start.59 = (bf16[128,1024]{1,0:T(8,128)(2,1)S(1)}, bf16[128,1024]{1,0:T(8,128)(2,1)S(1)}, u32[]{:S(2)}, u32[]{:S(2)}) collective-permute-start(bf16[128,1024]{1,0:T(8,128)(2,1)S(1)} %slice.240), channel_id=1, source_target_pairs={{0,8},{4,12},{8,0},{12,4},{1,9},{5,13},{9,1},{13,5},{2,10},{6,14},... | collective-permute-start | bytes 786440 | tf_op jit(solution)/shard_map/ppermute | solution.py:618
  (128 other events, 1615.6 us)
where the time goes:
time: 288 us; the launch traced here: 285 us
  waiting for transfers between devices  114 us (40%)
  starting transfers between devices  80.2 us (28%)
  Pallas kernels  40.2 us (14%)
  local copies, waits for them, and re-layouts  34.2 us (12%)
  other arithmetic  14 us (5%)
    ppermute x64, waiting for transfers between devices, send(): return lax.ppermute(x, axis, pairs)  114 us
    ppermute x64, starting transfers between devices, send(): return lax.ppermute(x, axis, pairs)  80.2 us
    pallas_call x16, Pallas kernels, kernel_call(): pl.pallas_call(run, out_shape=tuple((jax.ShapeDtypeStruct(s, d) for s, d...  40.2 us
    unnamed x185, local copies, waits for them, and re-layouts  20.8 us
  transfers between devices with their start and end apart: 64, of which 34 were waited for; matrix products, arithmetic and copies ran while one was open for 10% of the time, Pallas kernels for 12%

commit v1 on v0

--- a/solution.py
+++ b/solution.py
@@ -73,7 +73,7 @@
     return jnp.concatenate([jnp.where(first, pair, zero), jnp.where(first, zero, pair)], axis=0)
 
 
-def kernel_call(body, outs, cost, scalars, *operands, keep=False):
+def kernel_call(body, outs, cost, scalars, *operands, keep=False, near=False):
     flops, traffic, exps = cost
     flat, in_specs, scratch, plan = [], [], [], []
     if scalars is not None:
@@ -83,7 +83,7 @@
         parts = operand if isinstance(operand, list) else [operand]
         plan.append((len(flat), len(parts), isinstance(operand, list)))
         flat += parts
-        space = pltpu.HBM if isinstance(operand, list) else pltpu.VMEM
+        space = pl.ANY if isinstance(operand, list) and not near else pltpu.VMEM
         in_specs += [pl.BlockSpec(memory_space=space)] * len(parts)
         if isinstance(operand, list):
             whole = (sum(v.shape[0] for v in parts), parts[0].shape[1])
@@ -537,10 +537,10 @@
 
 def gate_back(
     heads, total_heads, count, cross_ref, sums_ref, dnormed_ref, gated_ref, gain_ref, zq_ref, y_ref, cum_ref,
-    bc_ref, *refs,
+    bc_ref, dq_ref, *refs,
 ):
     msgs, kv = refs[: count - 1], refs[count - 1 : 2 * count - 1]
-    dy_ref, dz_ref = refs[2 * count - 1 : 2 * count + 1]
+    dy_ref, dzq_ref = refs[2 * count - 1 : 2 * count + 1]
     sent = refs[2 * count + 1 :]
     width = y_ref.shape[1]
     size = total_heads * PM
@@ -551,7 +551,8 @@
     sig = sigmoid(z)
     dy = dgated * (z * sig)
     dy_ref[...] = dy
-    dz_ref[...] = low(dgated * y_ref[...] * sig * (1.0 + z * (1.0 - sig)))
+    dz = low(dgated * y_ref[...] * sig * (1.0 + z * (1.0 - sig)))
+    dzq_ref[...] = jnp.concatenate([dz, dq_ref[...]], axis=1)
     weighted = dy * mm(jnp.exp(cum_ref[...]), head_lanes(heads), HIGHEST)
     state = mm_tn(low(bc_ref[:, NS:]), low(weighted))
     for j in range(count):
@@ -743,17 +744,22 @@
     if direct():
         order = [((dp + i) % 2) * row_n + (row ^ x) for i in range(2) for x in (0, 2, 1, 3)]
         across, beside = swap(shard_in, "row", 2), swap(shard_in, "row", 1)
-        own, mix_own = swap(shard_in, "dp", 1), swap(shard_mix, "dp", 1)
-        across, beside, own, mix_own, hidden_ext = after_all(across, beside, own, mix_own, hidden_ext)
+        own = swap(shard_in, "dp", 1)
+        across, beside, own, hidden_ext, shard_ff = after_all(across, beside, own, hidden_ext, shard_ff)
         corner = swap(across, "row", 1)
         over = [swap(across, "dp", 1), swap(beside, "dp", 1)]
-        corner, shard_mix, shard_ff, *over = after_all(corner, shard_mix, shard_ff, *over)
+        ff_across = swap(shard_ff, "row", 2)
+        corner, ff_across, shard_mix, shard_ff, *over = after_all(corner, ff_across, shard_mix, shard_ff, *over)
         last = swap(corner, "dp", 1)
         mix_across, mix_beside = swap(shard_mix, "row", 2), swap(shard_mix, "row", 1)
-        ff_own = swap(shard_ff, "dp", 1)
-        last, mix_across, mix_beside, ff_own = after_all(last, mix_across, mix_beside, ff_own)
+        ff_beside = swap(shard_ff, "row", 1)
+        mix_own, ff_own = swap(shard_mix, "dp", 1), swap(shard_ff, "dp", 1)
+        last, mix_across, mix_beside, ff_beside, mix_own, ff_own = after_all(
+            last, mix_across, mix_beside, ff_beside, mix_own, ff_own
+        )
         in_blocks = [shard_in, across, beside, corner, own] + over + [last]
         mix_corner = swap(mix_across, "row", 1)
+        mix_over = [swap(v, "dp", 1) for v in (mix_across, mix_beside)]
     else:
         in_blocks = [lax.all_gather(shard_in, ("dp", "row"), axis=0, tiled=True)]
         mix_blocks = [lax.all_gather(shard_mix, ("dp", "row"), axis=0, tiled=True)]
@@ -803,19 +809,18 @@
         sin_kv,
         in_blocks,
         keep=True,
+        near=True,
     )
     if direct():
-        msg, mix_corner, mix_across, mix_beside, shard_ff = after_all(
-            msg, mix_corner, mix_across, mix_beside, shard_ff
-        )
+        msg, mix_corner, ff_across, *mix_over = after_all(msg, mix_corner, ff_across, *mix_over)
         msgs = [from_earlier(msg, j) for j in range(1, row_n)]
-        mix_over = [swap(v, "dp", 1) for v in (mix_across, mix_beside, mix_corner)]
-        ff_across, ff_beside = swap(shard_ff, "row", 2), swap(shard_ff, "row", 1)
-        ff_across, ff_beside, *moved = after_all(ff_across, ff_beside, *mix_over, *msgs)
+        mix_over.append(swap(mix_corner, "dp", 1))
+        ff_over = [swap(ff_across, "dp", 1)]
+        ff_across, ff_beside, ff_over[0], *moved = after_all(ff_across, ff_beside, ff_over[0], *mix_over, *msgs)
         mix_over, msgs = moved[:3], moved[3:]
+        mix_blocks = [shard_mix, mix_across, mix_beside, mix_corner, mix_own] + mix_over
         ff_corner = swap(ff_across, "row", 1)
-        ff_over = [swap(v, "dp", 1) for v in (ff_across, ff_beside)]
-        mix_blocks = [shard_mix, mix_across, mix_beside, mix_corner, mix_own] + mix_over
+        ff_over.append(swap(ff_beside, "dp", 1))
     else:
         msgs = [from_earlier(msg, j) for j in range(1, row_n)]
     zq, mix_full = kernel_call(
@@ -941,6 +946,9 @@
         mix_full,
     )
     cross = tiny_col_sum(cross)
+    if direct():
+        ff_got.append(swap(after(ff_parts[1][:near], grad_mix), "dp", 1))
+        cross, ff_got[0] = after_all(cross, ff_got[0])
     grad_query, grad_kv_own, *kv_sent = kernel_call(
         attend_back,
         (((rows, q_width), BF16), ((rows, LANES), F32)) + (((2 * part, width), BF16),) * (row_n - 1),
@@ -954,9 +962,9 @@
         key,
         value,
     )
-    grad_y, grad_z, *sent = kernel_call(
+    grad_y, grad_zq, *sent = kernel_call(
         partial(gate_back, heads, total_heads, row_n - 1),
-        (((rows, width), F32), ((rows, width), BF16)) + (((NS + 2 * part, width), BF16),) * (row_n - 1),
+        (((rows, width), F32), ((rows, width + q_width), BF16)) + (((NS + 2 * part, width), BF16),) * (row_n - 1),
         (2 * rows * NS * width, 4000000, rows * width),
         None,
         cross,
@@ -968,12 +976,11 @@
         y,
         cum,
         bc_map,
+        grad_query,
         *msgs[: row_n - 2],
         *kv_sent,
     )
     got = [from_later(sent[j - 1], j) for j in range(1, row_n)]
-    if direct():
-        ff_got.append(swap(after(ff_parts[1][:near], grad_y), "dp", 1))
     dx_local, dbc_local, dcum, dstep, dskip = kernel_call(
         partial(scan_back_local, heads),
         (
@@ -994,11 +1001,10 @@
         state_in,
         skip,
     )
-    grad_zq = jnp.concatenate([grad_z, grad_query], axis=1)
     act = jnp.concatenate([mamba_normed, attn_value], axis=1)
     mix_parts = weight_grad(hidden_in, grad_zq, grad_mix, act)
     mix_got = scatter_first(mix_parts)
-    got = list(after(tuple(got), mix_parts, ff_got[0]))
+    got = list(after(tuple(got), mix_parts, mix_got[0]))
 
     dpre, first, grad_dt, grad_kv, dsmall, dtaps = kernel_call(
         partial(scan_back_end, heads, row_n - 1),
@@ -1030,7 +1036,7 @@
         sin_kv,
     )
     following = from_later(first, 1)
-    following = after(following, ff_got)
+    following = after(following, ff_got, mix_got)
     ff_beside = scatter_beside(ff_parts, [after(ff_got[0], following)])
 
     grad_all, small, keep, give, _ = kernel_call(
@@ -1055,8 +1061,7 @@
         mix_full,
     )
     tail_width = conv_width + LANES
-    tail_parts = weight_grad(hidden_in, after(grad_all, mix_got[0])[:, :tail_width])
-    mix_got = mix_got[:1] + [after(v, *tail_parts) for v in mix_got[1:]]
+    tail_parts = weight_grad(hidden_in, grad_all[:, :tail_width])
     tail_got = scatter_first(tail_parts)
     mix_beside = scatter_beside(mix_parts, [after(mix_got[0], ff_beside, tail_got)])
     total, other = col_sum(keep, give)

time: 288 us -> 278 us (0.965)
  starting transfers between devices: 80.2 us -> 73.4 us
    ppermute x64, starting transfers between devices: 80.2 us -> 73.4 us  [send(): return lax.ppermute(x, axis, pairs)]
    unnamed x185 -> x144, local copies, waits for them, and re-layouts: 20.8 us -> 22.3 us
  transfers between devices with their start and end apart: 64 -> 64, of which waited for: 34 -> 29; matrix products, arithmetic and copies ran while one was open for 10% -> 9% of each run, Pallas kernels for 12% -> 13%
where the time goes in v1:
time: 278 us; the launch traced here: 276 us
  waiting for transfers between devices  112 us (40%)
  starting transfers between devices  73.4 us (26%)
  Pallas kernels  40.7 us (15%)
  local copies, waits for them, and re-layouts  35.3 us (13%)
  other arithmetic  13.1 us (5%)
    ppermute x64, waiting for transfers between devices, send(): return lax.ppermute(x, axis, pairs)  112 us
    ppermute x64, starting transfers between devices, send(): return lax.ppermute(x, axis, pairs)  73.4 us
    pallas_call x16, Pallas kernels, kernel_call(): pl.pallas_call(run, out_shape=tuple((jax.ShapeDtypeStruct(s, d) for s, d...  40.7 us
    unnamed x144, local copies, waits for them, and re-layouts  22.3 us
  transfers between devices with their start and end apart: 64, of which 29 were waited for; matrix products, arithmetic and copies ran while one was open for 9% of the time, Pallas kernels for 13%

profile of v1, /device:TPU:0, one launch (start us, length us, event | category | flops | bytes accessed | tf_op | source)
XLA Modules:
  0.0 276.3 jit_solution(674383091346472283)
XLA Ops:
  3.5 4.1 %collective-permute-start = (bf16[128,896]{1,0:T(8,128)(2,1)S(1)}, bf16[128,896]{1,0:T(8,128)(2,1)S(1)}, u32[]{:S(2)}, u32[]{:S(2)}) collective-permute-start(bf16[128,896]{1,0:T(8,128)(2,1)S(1)} %concatenate.37.refs_7_), channel_id=1, source_target_pairs={{0,8},{4,12},{8,0},{12,4},{1,9},{5,13},{9,1},{13,5},{2,10},{6,14},... | collective-permute-start | bytes 688136 | tf_op jit(solution)/shard_map/ppermute | solution.py:619
  18.6 3.4 %collective-permute-start.5 = (bf16[128,1536]{1,0:T(8,128)(2,1)S(1)}, bf16[128,1536]{1,0:T(8,128)(2,1)}, u32[]{:S(2)}, u32[]{:S(2)}) collective-permute-start(bf16[128,1536]{1,0:T(8,128)(2,1)S(1)} %pad_maximum_fusion.1.refs_6_), channel_id=1, source_target_pairs={{0,8},{4,12},{8,0},{12,4},{1,9},{5,13},{9,1},{13,5},{2,10},{6,14},... | collective-permute-start | bytes 1179656 | tf_op jit(solution)/shard_map/ppermute | solution.py:619
  26.0 9.5 %collective-permute-done.4.refs_10_ = bf16[128,896]{1,0:T(8,128)(2,1)S(1)} collective-permute-done((bf16[128,896]{1,0:T(8,128)(2,1)S(1)}, bf16[128,896]{1,0:T(8,128)(2,1)S(1)}, u32[]{:S(2)}, u32[]{:S(2)}) %collective-permute-start.4) | collective-permute-done | bytes 229408 | tf_op jit(solution)/shard_map/ppermute | solution.py:619
  37.0 2.9 %collective-permute-done.5.refs_7_ = bf16[128,1536]{1,0:T(8,128)(2,1)} collective-permute-done((bf16[128,1536]{1,0:T(8,128)(2,1)S(1)}, bf16[128,1536]{1,0:T(8,128)(2,1)}, u32[]{:S(2)}, u32[]{:S(2)}) %collective-permute-start.5) | collective-permute-done | bytes 393248 | tf_op jit(solution)/shard_map/ppermute | solution.py:619
  51.0 13.0 %collective-permute-done.10.refs_4_ = bf16[128,1024]{1,0:T(8,128)(2,1)S(1)} collective-permute-done((bf16[128,1024]{1,0:T(8,128)(2,1)S(1)}, bf16[128,1024]{1,0:T(8,128)(2,1)S(1)}, u32[]{:S(2)}, u32[]{:S(2)}) %collective-permute-start.10) | collective-permute-done | bytes 262176 | tf_op jit(solution)/shard_map/ppermute | solution.py:619
  71.4 6.1 %shard_map.364 = (f32[256,384]{1,0:T(8,128)S(1)}, bf16[240,384]{1,0:T(8,128)(2,1)S(1)}, bf16[272,896]{1,0:T(8,128)(2,1)S(1)}, f32[256,384]{1,0:T(8,128)S(1)}, f3...) custom-call(s32[10]{0:T(128)S(1)} %stack.43.refs_0_, ...), custom_call_target="tpu_custom_call" | custom-call | flops 503316480 | bytes 4000000 | tf_op jit(solution)/shard_map/pallas_call | solution.py:120
  79.6 3.5 %collective-permute-start.19 = (bf16[240,384]{1,0:T(8,128)(2,1)S(1)}, bf16[240,384]{1,0:T(8,128)(2,1)S(1)}, u32[]{:S(2)}, u32[]{:S(2)}) collective-permute-start(bf16[240,384]{1,0:T(8,128)(2,1)S(1)} %get-tuple-element.158.refs_1_), channel_id=1, source_target_pairs={{0,4},{4,8},{8,12},{1,5},{5,9},{9,13},{2,6},{6,10},{10,14},{3,7},{... | collective-permute-start | bytes 552968 | tf_op jit(solution)/shard_map/ppermute | solution.py:619
  83.1 3.1 %collective-permute-start.20 = (bf16[240,384]{1,0:T(8,128)(2,1)S(1)}, bf16[240,384]{1,0:T(8,128)(2,1)S(1)}, u32[]{:S(2)}, u32[]{:S(2)}) collective-permute-start(bf16[240,384]{1,0:T(8,128)(2,1)S(1)} %get-tuple-element.158.refs_1_), channel_id=1, source_target_pairs={{0,8},{4,12},{1,9},{5,13},{2,10},{6,14},{3,11},{7,15},{16,24},{20,... | collective-permute-start | bytes 552968 | tf_op jit(solution)/shard_map/ppermute | solution.py:619
  88.0 3.4 %collective-permute-done.20.refs_3_.refs_11_ = bf16[240,384]{1,0:T(8,128)(2,1)S(1)} collective-permute-done((bf16[240,384]{1,0:T(8,128)(2,1)S(1)}, bf16[240,384]{1,0:T(8,128)(2,1)S(1)}, u32[]{:S(2)}, u32[]{:S(2)}) %collective-permute-start.20) | collective-permute-done | bytes 184352 | tf_op jit(solution)/shard_map/ppermute | solution.py:619
  91.4 3.7 %collective-permute-done.21.refs_4_ = bf16[240,384]{1,0:T(8,128)(2,1)S(1)} collective-permute-done((bf16[240,384]{1,0:T(8,128)(2,1)S(1)}, bf16[240,384]{1,0:T(8,128)(2,1)S(1)}, u32[]{:S(2)}, u32[]{:S(2)}) %collective-permute-start.21) | collective-permute-done | bytes 184352 | tf_op jit(solution)/shard_map/ppermute | solution.py:619
  101.8 3.3 %shard_map.366 = (bf16[256,128]{1,0:T(8,128)(2,1)S(1)}, bf16[512,1024]{1,0:T(8,128)(2,1)S(1)}, bf16[512,64]{1,0:T(8,128)(2,1)S(1)}, bf16[1024,64]{1,0:T(8,128)(2...) custom-call(s32[10]{0:T(128)S(1)} %stack.43.refs_0_, ...), custom_call_target="tpu_custom_call" | custom-call | flops 268435456 | bytes 6000000 | tf_op jit(solution)/shard_map/pallas_call | solution.py:120
  116.9 5.3 %collective-permute-done.27 = bf16[128,1024]{1,0:T(8,128)(2,1)S(1)} collective-permute-done((bf16[128,1024]{1,0:T(8,128)(2,1)S(1)}, bf16[128,1024]{1,0:T(8,128)(2,1)S(1)}, u32[]{:S(2)}, u32[]{:S(2)}) %collective-permute-start.27) | collective-permute-done | bytes 262176 | tf_op jit(solution)/shard_map/ppermute | solution.py:619
  122.4 3.9 %collective-permute-done.29.refs_13_ = bf16[128,1536]{1,0:T(8,128)(2,1)S(1)} collective-permute-done((bf16[128,1536]{1,0:T(8,128)(2,1)S(1)}, bf16[128,1536]{1,0:T(8,128)(2,1)S(1)}, u32[]{:S(2)}, u32[]{:S(2)}) %collective-permute-start.29) | collective-permute-done | bytes 393248 | tf_op jit(solution)/shard_map/ppermute | solution.py:619
  126.3 5.4 %shard_map.368 = (f32[256,1024]{1,0:T(8,128)S(1)}, bf16[256,1024]{1,0:T(8,128)(2,1)S(1)}, bf16[256,1024]{1,0:T(8,128)(2,1)S(1)}, bf16[256,512]{1,0:T(8,128)(2,1)...) custom-call(s32[10]{0:T(128)S(1)} %stack.43.refs_0_, ...), custom_call_target="tpu_custom_call" | custom-call | flops 1879048192 | bytes 8000000 | tf_op jit(solution)/shard_map/pallas_call | solution.py:120
  138.0 5.7 %collective-permute-done.31 = bf16[128,1024]{1,0:T(8,128)(2,1)S(1)} collective-permute-done((bf16[128,1024]{1,0:T(8,128)(2,1)S(1)}, bf16[128,1024]{1,0:T(8,128)(2,1)S(1)}, u32[]{:S(2)}, u32[]{:S(2)}) %collective-permute-start.31) | collective-permute-done | bytes 262176 | tf_op jit(solution)/shard_map/ppermute | solution.py:619
  145.3 3.0 %shard_map.370 = (f32[256,1024]{1,0:T(8,128)S(1)}, bf16[256,1024]{1,0:T(8,128)(2,1)S(1)}, f32[8,1024]{1,0:T(8,128)S(1)}, f32[256,384]{1,0:T(8,128)S(1)}, bf16[25...) custom-call(s32[10]{0:T(128)S(1)} %stack.43.refs_0_, ...), custom_call_target="tpu_custom_call" | custom-call | flops 268435456 | bytes 6000000 | tf_op jit(solution)/shard_map/pallas_call | solution.py:120
  166.2 4.1 %collective-permute-done.36.refs_0_ = bf16[224,384]{1,0:T(8,128)(2,1)S(1)} collective-permute-done((bf16[224,384]{1,0:T(8,128)(2,1)S(1)}, bf16[224,384]{1,0:T(8,128)(2,1)S(1)}, u32[]{:S(2)}, u32[]{:S(2)}) %collective-permute-start.36) | collective-permute-done | bytes 172064 | tf_op jit(solution)/shard_map/ppermute | solution.py:619
  174.6 7.5 %collective-permute-done.37.refs_1_ = bf16[224,384]{1,0:T(8,128)(2,1)S(1)} collective-permute-done((bf16[224,384]{1,0:T(8,128)(2,1)S(1)}, bf16[224,384]{1,0:T(8,128)(2,1)S(1)}, u32[]{:S(2)}, u32[]{:S(2)}) %collective-permute-start.37) | collective-permute-done | bytes 172064 | tf_op jit(solution)/shard_map/ppermute | solution.py:619
  191.5 4.1 %collective-permute-done.42 = bf16[256,1024]{1,0:T(8,128)(2,1)} collective-permute-done((bf16[256,1024]{1,0:T(8,128)(2,1)}, bf16[256,1024]{1,0:T(8,128)(2,1)}, u32[]{:S(2)}, u32[]{:S(2)}) %collective-permute-start.42) | collective-permute-done | bytes 524320 | tf_op jit(solution)/shard_map/ppermute | solution.py:619
  201.1 3.1 %shard_map.376 = (bf16[256,896]{1,0:T(8,128)(2,1)S(1)}, f32[8,1664]{1,0:T(8,128)S(1)}, f32[128,1024]{1,0:T(8,128)S(1)}, bf16[128,1024]{1,0:T(8,128)(2,1)S(1)}, f32[256,1024]{1,0:T(8,128)}) custom-call(s32[10]{0:T(128)S(1)} %stack.43.refs_0_, f32[256,640]{1,0:T(8,128)S(1)} %copy-done.12, f32[8,640]{1,0:T(8,128)} %collective-permute-done.40.refs_2_, ...), custom_call_target="tpu_custom_call" | custom-call | flops 738197504 | bytes 8000000 | tf_op jit(solution)/shard_map/pallas_call | solution.py:120
  213.1 4.8 %collective-permute-done.44 = bf16[128,1024]{1,0:T(8,128)(2,1)S(1)} collective-permute-done((bf16[128,1024]{1,0:T(8,128)(2,1)S(1)}, bf16[128,1024]{1,0:T(8,128)(2,1)S(1)}, u32[]{:S(2)}, u32[]{:S(2)}) %collective-permute-start.44) | collective-permute-done | bytes 262176 | tf_op jit(solution)/shard_map/ppermute | solution.py:619
  233.4 8.4 %collective-permute-done.53 = bf16[256,768]{1,0:T(8,128)(2,1)S(1)} collective-permute-done((bf16[256,768]{1,0:T(8,128)(2,1)S(1)}, bf16[256,768]{1,0:T(8,128)(2,1)S(1)}, u32[]{:S(2)}, u32[]{:S(2)}) %collective-permute-start.53) | collective-permute-done | bytes 393248 | tf_op jit(solution)/shard_map/ppermute | solution.py:619
  250.2 6.1 %collective-permute-done.55 = f32[8,1664]{1,0:T(8,128)S(1)} collective-permute-done((f32[8,1664]{1,0:T(8,128)S(1)}, f32[8,1664]{1,0:T(8,128)S(1)}, u32[]{:S(2)}, u32[]{:S(2)}) %collective-permute-start.55) | collective-permute-done | bytes 53280 | tf_op jit(solution)/shard_map/ppermute | solution.py:619
  269.2 3.5 %collective-permute-done.59 = bf16[128,1024]{1,0:T(8,128)(2,1)S(1)} collective-permute-done((bf16[128,1024]{1,0:T(8,128)(2,1)S(1)}, bf16[128,1024]{1,0:T(8,128)(2,1)S(1)}, u32[]{:S(2)}, u32[]{:S(2)}) %collective-permute-start.59) | collective-permute-done | bytes 262176 | tf_op jit(solution)/shard_map/ppermute | solution.py:619
  (346 shorter events, 153.7 us)
Async XLA Ops:
  3.5 15.1 %collective-permute-start = (bf16[128,896]{1,0:T(8,128)(2,1)S(1)}, bf16[128,896]{1,0:T(8,128)(2,1)S(1)}, u32[]{:S(2)}, u32[]{:S(2)}) collective-permute-start(bf16[128,896]{1,0:T(8,128)(2,1)S(1)} %concatenate.37.refs_7_), channel_id=1, source_target_pairs={{0,8},{4,12},{8,0},{12,4},{1,9},{5,13},{9,1},{13,5},{2,10},{6,14},... | collective-permute-start | bytes 688136 | tf_op jit(solution)/shard_map/ppermute | solution.py:619
  18.6 21.2 %collective-permute-start.5 = (bf16[128,1536]{1,0:T(8,128)(2,1)S(1)}, bf16[128,1536]{1,0:T(8,128)(2,1)}, u32[]{:S(2)}, u32[]{:S(2)}) collective-permute-start(bf16[128,1536]{1,0:T(8,128)(2,1)S(1)} %pad_maximum_fusion.1.refs_6_), channel_id=1, source_target_pairs={{0,8},{4,12},{8,0},{12,4},{1,9},{5,13},{9,1},{13,5},{2,10},{6,14},... | collective-permute-start | bytes 1179656 | tf_op jit(solution)/shard_map/ppermute | solution.py:619
  42.1 21.9 %collective-permute-start.11 = (bf16[128,1536]{1,0:T(8,128)(2,1)S(1)}, bf16[128,1536]{1,0:T(8,128)(2,1)}, u32[]{:S(2)}, u32[]{:S(2)}) collective-permute-start(bf16[128,1536]{1,0:T(8,128)(2,1)S(1)} %pad_maximum_fusion.1.refs_6_), channel_id=1, source_target_pairs={{0,4},{4,0},{8,12},{12,8},{1,5},{5,1},{9,13},{13,9},{2,6},{6,2},{1... | collective-permute-start | bytes 1179656 | tf_op jit(solution)/shard_map/ppermute | solution.py:619
  42.2 21.8 %collective-permute-start.13 = (bf16[128,1536]{1,0:T(8,128)(2,1)S(1)}, bf16[128,1536]{1,0:T(8,128)(2,1)}, u32[]{:S(2)}, u32[]{:S(2)}) collective-permute-start(bf16[128,1536]{1,0:T(8,128)(2,1)S(1)} %pad_maximum_fusion.1.refs_6_), channel_id=1, source_target_pairs={{0,16},{16,0},{1,17},{17,1},{2,18},{18,2},{3,19},{19,3},{4,20},{20... | collective-permute-start | bytes 1179656 | tf_op jit(solution)/shard_map/ppermute | solution.py:619
  42.8 21.2 %collective-permute-start.10 = (bf16[128,1024]{1,0:T(8,128)(2,1)S(1)}, bf16[128,1024]{1,0:T(8,128)(2,1)S(1)}, u32[]{:S(2)}, u32[]{:S(2)}) collective-permute-start(bf16[128,1024]{1,0:T(8,128)(2,1)S(1)} %pad_maximum_fusion.2.refs_2_), channel_id=1, source_target_pairs={{0,4},{4,0},{8,12},{12,8},{1,5},{5,1},{9,13},{13,9},{2,6},{6,2},{1... | collective-permute-start | bytes 786440 | tf_op jit(solution)/shard_map/ppermute | solution.py:619
  44.8 19.2 %collective-permute-start.12 = (bf16[128,1024]{1,0:T(8,128)(2,1)S(1)}, bf16[128,1024]{1,0:T(8,128)(2,1)S(1)}, u32[]{:S(2)}, u32[]{:S(2)}) collective-permute-start(bf16[128,1024]{1,0:T(8,128)(2,1)S(1)} %pad_maximum_fusion.2.refs_2_), channel_id=1, source_target_pairs={{0,16},{16,0},{1,17},{17,1},{2,18},{18,2},{3,19},{19,3},{4,20},{20... | collective-permute-start | bytes 786440 | tf_op jit(solution)/shard_map/ppermute | solution.py:619
  49.0 15.0 %collective-permute-start.9 = (bf16[128,1024]{1,0:T(8,128)(2,1)S(1)}, bf16[128,1024]{1,0:T(8,128)(2,1)S(1)}, u32[]{:S(2)}, u32[]{:S(2)}) collective-permute-start(bf16[128,1024]{1,0:T(8,128)(2,1)S(1)} %pad_maximum_fusion.2.refs_2_), channel_id=1, source_target_pairs={{0,8},{4,12},{8,0},{12,4},{1,9},{5,13},{9,1},{13,5},{2,10},{6,14},... | collective-permute-start | bytes 786440 | tf_op jit(solution)/shard_map/ppermute | solution.py:619
  77.5 17.6 %collective-permute-start.17 = (bf16[128,1536]{1,0:T(8,128)(2,1)}, bf16[128,1536]{1,0:T(8,128)(2,1)S(1)}, u32[]{:S(2)}, u32[]{:S(2)}) collective-permute-start(bf16[128,1536]{1,0:T(8,128)(2,1)} %collective-permute-done.5.refs_7_), channel_id=1, source_target_pairs={{0,16},{16,0},{1,17},{17,1},{2,18},{18,2},{3,19},{19,3},{4,20},{20... | collective-permute-start | bytes 1179656 | tf_op jit(solution)/shard_map/ppermute | solution.py:619
  78.1 17.0 %collective-permute-start.18 = (bf16[128,1024]{1,0:T(8,128)(2,1)S(1)}, bf16[128,1024]{1,0:T(8,128)(2,1)S(1)}, u32[]{:S(2)}, u32[]{:S(2)}) collective-permute-start(bf16[128,1024]{1,0:T(8,128)(2,1)S(1)} %collective-permute-done.14.refs_5_), channel_id=1, source_target_pairs={{0,16},{16,0},{1,17},{17,1},{2,18},{18,2},{3,19},{19,3},{4,20},{20... | collective-permute-start | bytes 786440 | tf_op jit(solution)/shard_map/ppermute | solution.py:619
  95.1 17.1 %collective-permute-start.24 = (bf16[128,1536]{1,0:T(8,128)(2,1)}, bf16[128,1536]{1,0:T(8,128)(2,1)S(1)}, u32[]{:S(2)}, u32[]{:S(2)}) collective-permute-start(bf16[128,1536]{1,0:T(8,128)(2,1)} %collective-permute-done.5.refs_7_), channel_id=1, source_target_pairs={{0,4},{4,0},{8,12},{12,8},{1,5},{5,1},{9,13},{13,9},{2,6},{6,2},{1... | collective-permute-start | bytes 1179656 | tf_op jit(solution)/shard_map/ppermute | solution.py:619
  97.2 15.0 %collective-permute-start.25 = (bf16[128,1536]{1,0:T(8,128)(2,1)}, bf16[128,1536]{1,0:T(8,128)(2,1)S(1)}, u32[]{:S(2)}, u32[]{:S(2)}) collective-permute-start(bf16[128,1536]{1,0:T(8,128)(2,1)} %collective-permute-done.11.refs_8_), channel_id=1, source_target_pairs={{0,16},{16,0},{1,17},{17,1},{2,18},{18,2},{3,19},{19,3},{4,20},{20... | collective-permute-start | bytes 1179656 | tf_op jit(solution)/shard_map/ppermute | solution.py:619
  136.5 20.4 %collective-permute-start.35 = (bf16[256,1536]{1,0:T(8,128)(2,1)S(1)}, bf16[256,1536]{1,0:T(8,128)(2,1)S(1)}, u32[]{:S(2)}, u32[]{:S(2)}) collective-permute-start(bf16[256,1536]{1,0:T(8,128)(2,1)S(1)} %get-tuple-element.287), channel_id=1, source_target_pairs={{0,16},{16,0},{1,17},{17,1},{2,18},{18,2},{3,19},{19,3},{4,20},{20... | collective-permute-start | bytes 2359304 | tf_op jit(solution)/shard_map/ppermute | solution.py:619
  149.5 46.2 %collective-permute-start.41 = (bf16[256,1536]{1,0:T(8,128)(2,1)}, bf16[256,1536]{1,0:T(8,128)(2,1)}, u32[]{:S(2)}, u32[]{:S(2)}) collective-permute-start(bf16[256,1536]{1,0:T(8,128)(2,1)} %get-tuple-element.239), channel_id=1, source_target_pairs={{0,16},{16,0},{1,17},{17,1},{2,18},{18,2},{3,19},{19,3},{4,20},{20... | collective-permute-start | bytes 2359304 | tf_op jit(solution)/shard_map/ppermute | solution.py:619
  160.9 24.0 %collective-permute-start.39 = (bf16[256,1024]{1,0:T(8,128)(2,1)S(1)}, bf16[256,1024]{1,0:T(8,128)(2,1)S(1)}, u32[]{:S(2)}, u32[]{:S(2)}) collective-permute-start(bf16[256,1024]{1,0:T(8,128)(2,1)S(1)} %get-tuple-element.289), channel_id=1, source_target_pairs={{0,16},{16,0},{1,17},{17,1},{2,18},{18,2},{3,19},{19,3},{4,20},{20... | collective-permute-start | bytes 1572872 | tf_op jit(solution)/shard_map/ppermute | solution.py:619
  163.8 31.8 %collective-permute-start.42 = (bf16[256,1024]{1,0:T(8,128)(2,1)}, bf16[256,1024]{1,0:T(8,128)(2,1)}, u32[]{:S(2)}, u32[]{:S(2)}) collective-permute-start(bf16[256,1024]{1,0:T(8,128)(2,1)} %get-tuple-element.288), channel_id=1, source_target_pairs={{0,16},{16,0},{1,17},{17,1},{2,18},{18,2},{3,19},{19,3},{4,20},{20... | collective-permute-start | bytes 1572872 | tf_op jit(solution)/shard_map/ppermute | solution.py:619
  164.9 17.2 %collective-permute-start.37 = (bf16[224,384]{1,0:T(8,128)(2,1)S(1)}, bf16[224,384]{1,0:T(8,128)(2,1)S(1)}, u32[]{:S(2)}, u32[]{:S(2)}) collective-permute-start(bf16[224,384]{1,0:T(8,128)(2,1)S(1)} %get-tuple-element.214), channel_id=1, source_target_pairs={{8,0},{12,4},{9,1},{13,5},{10,2},{14,6},{11,3},{15,7},{24,16},{28,... | collective-permute-start | bytes 516104 | tf_op jit(solution)/shard_map/ppermute | solution.py:619
  197.2 21.3 %collective-permute-start.52 = (bf16[256,1536]{1,0:T(8,128)(2,1)S(1)}, bf16[256,1536]{1,0:T(8,128)(2,1)S(1)}, u32[]{:S(2)}, u32[]{:S(2)}) collective-permute-start(bf16[256,1536]{1,0:T(8,128)(2,1)S(1)} %add_convert_fusion), channel_id=1, source_target_pairs={{0,4},{4,0},{8,12},{12,8},{1,5},{5,1},{9,13},{13,9},{2,6},{6,2},{1... | collective-permute-start | bytes 2359304 | tf_op jit(solution)/shard_map/ppermute | solution.py:619
  207.7 18.0 %collective-permute-start.57 = (bf16[256,768]{1,0:T(8,128)(2,1)S(1)}, bf16[256,768]{1,0:T(8,128)(2,1)S(1)}, u32[]{:S(2)}, u32[]{:S(2)}) collective-permute-start(bf16[256,768]{1,0:T(8,128)(2,1)S(1)} %get-tuple-element.293), channel_id=1, source_target_pairs={{0,16},{16,0},{1,17},{17,1},{2,18},{18,2},{3,19},{19,3},{4,20},{20... | collective-permute-start | bytes 1179656 | tf_op jit(solution)/shard_map/ppermute | solution.py:619
  220.0 23.3 %collective-permute-start.63 = (bf16[128,1536]{1,0:T(8,128)(2,1)S(1)}, bf16[128,1536]{1,0:T(8,128)(2,1)S(1)}, u32[]{:S(2)}, u32[]{:S(2)}) collective-permute-start(bf16[128,1536]{1,0:T(8,128)(2,1)S(1)} %slice.239), channel_id=1, source_target_pairs={{0,8},{4,12},{8,0},{12,4},{1,9},{5,13},{9,1},{13,5},{2,10},{6,14},... | collective-permute-start | bytes 1179656 | tf_op jit(solution)/shard_map/ppermute | solution.py:619
  221.7 20.1 %collective-permute-start.53 = (bf16[256,768]{1,0:T(8,128)(2,1)S(1)}, bf16[256,768]{1,0:T(8,128)(2,1)S(1)}, u32[]{:S(2)}, u32[]{:S(2)}) collective-permute-start(bf16[256,768]{1,0:T(8,128)(2,1)S(1)} %add_convert_fusion.2), channel_id=1, source_target_pairs={{0,4},{4,0},{8,12},{12,8},{1,5},{5,1},{9,13},{13,9},{2,6},{6,2},{1... | collective-permute-start | bytes 1179656 | tf_op jit(solution)/shard_map/ppermute | solution.py:619
  228.3 28.5 %collective-permute-start.58 = (bf16[256,1024]{1,0:T(8,128)(2,1)}, bf16[256,1024]{1,0:T(8,128)(2,1)}, u32[]{:S(2)}, u32[]{:S(2)}) collective-permute-start(bf16[256,1024]{1,0:T(8,128)(2,1)} %add_convert_fusion.1), channel_id=1, source_target_pairs={{0,4},{4,0},{8,12},{12,8},{1,5},{5,1},{9,13},{13,9},{2,6},{6,2},{1... | collective-permute-start | bytes 1572872 | tf_op jit(solution)/shard_map/ppermute | solution.py:619
  233.3 27.6 %collective-permute-start.47 = (bf16[128,1024]{1,0:T(8,128)(2,1)S(1)}, bf16[128,1024]{1,0:T(8,128)(2,1)S(1)}, u32[]{:S(2)}, u32[]{:S(2)}) collective-permute-start(bf16[128,1024]{1,0:T(8,128)(2,1)S(1)} %add_convert_fusion.3.refs_1_), channel_id=1, source_target_pairs={{0,1},{1,0},{2,3},{3,2},{4,5},{5,4},{6,7},{7,6},{8,9},{9,8},{10,11... | collective-permute-start | bytes 786440 | tf_op jit(solution)/shard_map/ppermute | solution.py:619
  248.0 15.8 %collective-permute-start.60 = (bf16[128,768]{1,0:T(8,128)(2,1)S(1)}, bf16[128,768]{1,0:T(8,128)(2,1)S(1)}, u32[]{:S(2)}, u32[]{:S(2)}) collective-permute-start(bf16[128,768]{1,0:T(8,128)(2,1)S(1)} %slice.241), channel_id=1, source_target_pairs={{0,8},{4,12},{8,0},{12,4},{1,9},{5,13},{9,1},{13,5},{2,10},{6,14},... | collective-permute-start | bytes 589832 | tf_op jit(solution)/shard_map/ppermute | solution.py:619
  258.3 14.3 %collective-permute-start.59 = (bf16[128,1024]{1,0:T(8,128)(2,1)S(1)}, bf16[128,1024]{1,0:T(8,128)(2,1)S(1)}, u32[]{:S(2)}, u32[]{:S(2)}) collective-permute-start(bf16[128,1024]{1,0:T(8,128)(2,1)S(1)} %slice.240), channel_id=1, source_target_pairs={{0,8},{4,12},{8,0},{12,4},{1,9},{5,13},{9,1},{13,5},{2,10},{6,14},... | collective-permute-start | bytes 786440 | tf_op jit(solution)/shard_map/ppermute | solution.py:619
  (108 other events, 1027.6 us)

commit v2 on v1

--- a/solution.py
+++ b/solution.py
@@ -664,12 +664,13 @@
     return swap(low(parts[0][half:].astype(F32) + got[0].astype(F32)), "row", 1)
 
 
-def scatter_last(parts, got, beside):
+def scatter_last(parts, got, beside, *late):
     if len(parts) == 1:
         return beside.astype(F32)
     blk = parts[0].shape[0] // 4
     total = parts[0][: 2 * blk].astype(F32) + got[1].astype(F32) + beside.astype(F32)
-    return total[:blk] + swap(low(total[blk:]), "row", 2).astype(F32)
+    across = swap(low(total[blk:]), "row", 2)
+    return total[:blk] + (after(across, *late) if late else across).astype(F32)
 
 
 def col_sum(keep, give, *others):
@@ -691,11 +692,12 @@
     return values + swap(values, "col", 2)
 
 
-def tiny_row_sum(values):
+def tiny_row_sum(values, before_rows):
     if lax.axis_size("dp") == 2:
         values = values + swap(values, "dp", 1)
     else:
         values = lax.psum(values, "dp")
+    values = after(values, before_rows)
     values = values + swap(values, "row", 1)
     return values + swap(values, "row", 2)
 
@@ -1036,8 +1038,8 @@
         sin_kv,
     )
     following = from_later(first, 1)
-    following = after(following, ff_got, mix_got)
-    ff_beside = scatter_beside(ff_parts, [after(ff_got[0], following)])
+    ff_beside = scatter_beside(ff_parts, [after(ff_got[0], got[0])])
+    following = after(following, ff_got, mix_got, ff_beside)
 
     grad_all, small, keep, give, _ = kernel_call(
         conv_and_input_back,
@@ -1065,7 +1067,6 @@
     tail_got = scatter_first(tail_parts)
     mix_beside = scatter_beside(mix_parts, [after(mix_got[0], ff_beside, tail_got)])
     total, other = col_sum(keep, give)
-    grad_ff = scatter_last(ff_parts, ff_got, after(ff_beside, tail_got[0]))
     out_total, out_other = col_sum(out_keep, after(out_give, total))
     layer_out, _ = kernel_call(
         output_sum,
@@ -1078,7 +1079,8 @@
     )
     tail_beside = scatter_beside(tail_parts, [after(tail_got[0], ff_beside)])
     grad_in_w = scatter_last(tail_parts, tail_got, tail_beside)
-    grad_mix_w = scatter_last(mix_parts, mix_got, after(mix_beside, tail_beside))
+    grad_ff = scatter_last(ff_parts, ff_got, after(ff_beside, grad_all), tail_beside)
+    grad_mix_w = scatter_last(mix_parts, mix_got, after(mix_beside, tail_beside), grad_in_w)
     grad_tokens, _ = kernel_call(
         input_back,
         (((rows, model), F32), full_scratch),
@@ -1103,7 +1105,7 @@
     lane = lax.broadcasted_iota(jnp.int32, small.shape, 1)
     partial_lanes = ((line == 7) & (lane < model)) | ((line < KC) & (lane >= model + width))
     small = jnp.where(partial_lanes, tiny_col_sum(small), small)
-    small = tiny_row_sum(after(small, tail_beside))
+    small = tiny_row_sum(small, grad_in_w)
     taps_at = model + width
     place = (dp * row_n + row) * blk
     return (

time: 278 us -> 277 us (level)
  waiting for transfers between devices: 112 us -> 120 us
  local copies, waits for them, and re-layouts: 35.3 us -> 28 us
    ppermute x64, waiting for transfers between devices: 112 us -> 120 us  [send(): return lax.ppermute(x, axis, pairs)]
    unnamed x144 -> x106, local copies, waits for them, and re-layouts: 22.3 us -> 15.5 us
  transfers between devices with their start and end apart: 64 -> 64, of which waited for: 29 -> 28; matrix products, arithmetic and copies ran while one was open for 9% -> 11% of each run, Pallas kernels for 13% -> 10%
where the time goes in v2:
time: 277 us; the launch traced here: 276 us
  waiting for transfers between devices  120 us (43%)
  starting transfers between devices  70.8 us (26%)
  Pallas kernels  40.8 us (15%)
  local copies, waits for them, and re-layouts  28 us (10%)
  other arithmetic  14.4 us (5%)
    ppermute x64, waiting for transfers between devices, send(): return lax.ppermute(x, axis, pairs)  120 us
    ppermute x64, starting transfers between devices, send(): return lax.ppermute(x, axis, pairs)  70.8 us
    pallas_call x16, Pallas kernels, kernel_call(): pl.pallas_call(run, out_shape=tuple((jax.ShapeDtypeStruct(s, d) for s, d...  40.8 us
    unnamed x106, local copies, waits for them, and re-layouts  15.5 us
  transfers between devices with their start and end apart: 64, of which 28 were waited for; matrix products, arithmetic and copies ran while one was open for 11% of the time, Pallas kernels for 10%

profile of v2, /device:TPU:0, one launch (start us, length us, event | category | flops | bytes accessed | tf_op | source)
XLA Modules:
  0.0 275.7 jit_solution(2423269727268618735)
XLA Ops:
  3.5 4.1 %collective-permute-start = (bf16[128,896]{1,0:T(8,128)(2,1)S(1)}, bf16[128,896]{1,0:T(8,128)(2,1)S(1)}, u32[]{:S(2)}, u32[]{:S(2)}) collective-permute-start(bf16[128,896]{1,0:T(8,128)(2,1)S(1)} %concatenate.37.refs_7_), channel_id=1, source_target_pairs={{0,8},{4,12},{8,0},{12,4},{1,9},{5,13},{9,1},{13,5},{2,10},{6,14},... | collective-permute-start | bytes 688136 | tf_op jit(solution)/shard_map/ppermute | solution.py:619
  18.6 3.4 %collective-permute-start.5 = (bf16[128,1536]{1,0:T(8,128)(2,1)S(1)}, bf16[128,1536]{1,0:T(8,128)(2,1)S(1)}, u32[]{:S(2)}, u32[]{:S(2)}) collective-permute-start(bf16[128,1536]{1,0:T(8,128)(2,1)S(1)} %pad_maximum_fusion.1.refs_6_), channel_id=1, source_target_pairs={{0,8},{4,12},{8,0},{12,4},{1,9},{5,13},{9,1},{13,5},{2,10},{6,14},... | collective-permute-start | bytes 1179656 | tf_op jit(solution)/shard_map/ppermute | solution.py:619
  26.1 9.5 %collective-permute-done.4.refs_10_ = bf16[128,896]{1,0:T(8,128)(2,1)S(1)} collective-permute-done((bf16[128,896]{1,0:T(8,128)(2,1)S(1)}, bf16[128,896]{1,0:T(8,128)(2,1)S(1)}, u32[]{:S(2)}, u32[]{:S(2)}) %collective-permute-start.4) | collective-permute-done | bytes 229408 | tf_op jit(solution)/shard_map/ppermute | solution.py:619
  51.1 12.7 %collective-permute-done.10.refs_4_ = bf16[128,1024]{1,0:T(8,128)(2,1)S(1)} collective-permute-done((bf16[128,1024]{1,0:T(8,128)(2,1)S(1)}, bf16[128,1024]{1,0:T(8,128)(2,1)S(1)}, u32[]{:S(2)}, u32[]{:S(2)}) %collective-permute-start.10) | collective-permute-done | bytes 262176 | tf_op jit(solution)/shard_map/ppermute | solution.py:619
  71.2 6.1 %shard_map.364 = (f32[256,384]{1,0:T(8,128)S(1)}, bf16[240,384]{1,0:T(8,128)(2,1)S(1)}, bf16[272,896]{1,0:T(8,128)(2,1)S(1)}, f32[256,384]{1,0:T(8,128)S(1)}, f3...) custom-call(s32[10]{0:T(128)S(1)} %stack.43.refs_0_, ...), custom_call_target="tpu_custom_call" | custom-call | flops 503316480 | bytes 4000000 | tf_op jit(solution)/shard_map/pallas_call | solution.py:120
  79.4 3.5 %collective-permute-start.19 = (bf16[240,384]{1,0:T(8,128)(2,1)S(1)}, bf16[240,384]{1,0:T(8,128)(2,1)S(1)}, u32[]{:S(2)}, u32[]{:S(2)}) collective-permute-start(bf16[240,384]{1,0:T(8,128)(2,1)S(1)} %get-tuple-element.160.refs_1_), channel_id=1, source_target_pairs={{0,4},{4,8},{8,12},{1,5},{5,9},{9,13},{2,6},{6,10},{10,14},{3,7},{... | collective-permute-start | bytes 552968 | tf_op jit(solution)/shard_map/ppermute | solution.py:619
  83.0 3.0 %collective-permute-start.20 = (bf16[240,384]{1,0:T(8,128)(2,1)S(1)}, bf16[240,384]{1,0:T(8,128)(2,1)S(1)}, u32[]{:S(2)}, u32[]{:S(2)}) collective-permute-start(bf16[240,384]{1,0:T(8,128)(2,1)S(1)} %get-tuple-element.160.refs_1_), channel_id=1, source_target_pairs={{0,8},{4,12},{1,9},{5,13},{2,10},{6,14},{3,11},{7,15},{16,24},{20,... | collective-permute-start | bytes 552968 | tf_op jit(solution)/shard_map/ppermute | solution.py:619
  87.9 3.4 %collective-permute-done.20.refs_3_.refs_11_ = bf16[240,384]{1,0:T(8,128)(2,1)S(1)} collective-permute-done((bf16[240,384]{1,0:T(8,128)(2,1)S(1)}, bf16[240,384]{1,0:T(8,128)(2,1)S(1)}, u32[]{:S(2)}, u32[]{:S(2)}) %collective-permute-start.20) | collective-permute-done | bytes 184352 | tf_op jit(solution)/shard_map/ppermute | solution.py:619
  91.3 4.0 %collective-permute-done.21.refs_4_ = bf16[240,384]{1,0:T(8,128)(2,1)S(1)} collective-permute-done((bf16[240,384]{1,0:T(8,128)(2,1)S(1)}, bf16[240,384]{1,0:T(8,128)(2,1)S(1)}, u32[]{:S(2)}, u32[]{:S(2)}) %collective-permute-start.21) | collective-permute-done | bytes 184352 | tf_op jit(solution)/shard_map/ppermute | solution.py:619
  98.8 3.3 %shard_map.366 = (bf16[256,128]{1,0:T(8,128)(2,1)S(1)}, bf16[512,1024]{1,0:T(8,128)(2,1)S(1)}, bf16[512,64]{1,0:T(8,128)(2,1)S(1)}, bf16[1024,64]{1,0:T(8,128)(2...) custom-call(s32[10]{0:T(128)S(1)} %stack.43.refs_0_, ...), custom_call_target="tpu_custom_call" | custom-call | flops 268435456 | bytes 6000000 | tf_op jit(solution)/shard_map/pallas_call | solution.py:120
  113.9 5.3 %collective-permute-done.27 = bf16[128,1024]{1,0:T(8,128)(2,1)S(1)} collective-permute-done((bf16[128,1024]{1,0:T(8,128)(2,1)S(1)}, bf16[128,1024]{1,0:T(8,128)(2,1)S(1)}, u32[]{:S(2)}, u32[]{:S(2)}) %collective-permute-start.27) | collective-permute-done | bytes 262176 | tf_op jit(solution)/shard_map/ppermute | solution.py:619
  119.3 3.9 %collective-permute-done.29.refs_13_ = bf16[128,1536]{1,0:T(8,128)(2,1)S(1)} collective-permute-done((bf16[128,1536]{1,0:T(8,128)(2,1)S(1)}, bf16[128,1536]{1,0:T(8,128)(2,1)S(1)}, u32[]{:S(2)}, u32[]{:S(2)}) %collective-permute-start.29) | collective-permute-done | bytes 393248 | tf_op jit(solution)/shard_map/ppermute | solution.py:619
  123.2 5.7 %shard_map.368 = (f32[256,1024]{1,0:T(8,128)S(1)}, bf16[256,1024]{1,0:T(8,128)(2,1)S(1)}, bf16[256,1024]{1,0:T(8,128)(2,1)S(1)}, bf16[256,512]{1,0:T(8,128)(2,1)...) custom-call(s32[10]{0:T(128)S(1)} %stack.43.refs_0_, ...), custom_call_target="tpu_custom_call" | custom-call | flops 1879048192 | bytes 8000000 | tf_op jit(solution)/shard_map/pallas_call | solution.py:120
  133.0 6.5 %collective-permute-done.31 = bf16[128,1024]{1,0:T(8,128)(2,1)S(1)} collective-permute-done((bf16[128,1024]{1,0:T(8,128)(2,1)S(1)}, bf16[128,1024]{1,0:T(8,128)(2,1)S(1)}, u32[]{:S(2)}, u32[]{:S(2)}) %collective-permute-start.31) | collective-permute-done | bytes 262176 | tf_op jit(solution)/shard_map/ppermute | solution.py:619
  141.1 3.1 %shard_map.370 = (f32[256,1024]{1,0:T(8,128)S(1)}, bf16[256,1024]{1,0:T(8,128)(2,1)S(1)}, f32[8,1024]{1,0:T(8,128)S(1)}, f32[256,384]{1,0:T(8,128)S(1)}, bf16[25...) custom-call(s32[10]{0:T(128)S(1)} %stack.43.refs_0_, ...), custom_call_target="tpu_custom_call" | custom-call | flops 268435456 | bytes 6000000 | tf_op jit(solution)/shard_map/pallas_call | solution.py:120
  162.2 12.7 %collective-permute-done.37.refs_1_ = bf16[224,384]{1,0:T(8,128)(2,1)S(1)} collective-permute-done((bf16[224,384]{1,0:T(8,128)(2,1)S(1)}, bf16[224,384]{1,0:T(8,128)(2,1)S(1)}, u32[]{:S(2)}, u32[]{:S(2)}) %collective-permute-start.37) | collective-permute-done | bytes 172064 | tf_op jit(solution)/shard_map/ppermute | solution.py:619
  182.4 12.3 %collective-permute-done.42 = bf16[256,1024]{1,0:T(8,128)(2,1)S(1)} collective-permute-done((bf16[256,1024]{1,0:T(8,128)(2,1)S(1)}, bf16[256,1024]{1,0:T(8,128)(2,1)S(1)}, u32[]{:S(2)}, u32[]{:S(2)}) %collective-permute-start.42) | collective-permute-done | bytes 524320 | tf_op jit(solution)/shard_map/ppermute | solution.py:619
  194.8 3.0 %shard_map.376 = (bf16[256,896]{1,0:T(8,128)(2,1)S(1)}, f32[8,1664]{1,0:T(8,128)S(1)}, f32[128,1024]{1,0:T(8,128)S(1)}, bf16[128,1024]{1,0:T(8,128)(2,1)S(1)}, f32[256,1024]{1,0:T(8,128)}) custom-call(s32[10]{0:T(128)S(1)} %stack.43.refs_0_, f32[256,640]{1,0:T(8,128)S(1)} %get-tuple-element.238.refs_1_, f32[8,640]{1,0:T(8,128)S(1)} %collective-permute-done.40.refs_2_, ...), custom_call_target="tpu_custom_call" | custom-call | flops 738197504 | bytes 8000000 | tf_op jit(solution)/shard_map/pallas_call | solution.py:120
  206.9 3.5 %collective-permute-start.63 = (bf16[128,1536]{1,0:T(8,128)(2,1)S(1)}, bf16[128,1536]{1,0:T(8,128)(2,1)S(1)}, u32[]{:S(2)}, u32[]{:S(2)}) collective-permute-start(bf16[128,1536]{1,0:T(8,128)(2,1)S(1)} %slice.239), channel_id=1, source_target_pairs={{0,8},{4,12},{8,0},{12,4},{1,9},{5,13},{9,1},{13,5},{2,10},{6,14},... | collective-permute-start | bytes 1179656 | tf_op jit(solution)/shard_map/ppermute | solution.py:619
  210.9 4.4 %collective-permute-done.52 = f32[8,1664]{1,0:T(8,128)S(1)} collective-permute-done((f32[8,1664]{1,0:T(8,128)S(1)}, f32[8,1664]{1,0:T(8,128)S(1)}, u32[]{:S(2)}, u32[]{:S(2)}) %collective-permute-start.52) | collective-permute-done | bytes 53280 | tf_op jit(solution)/shard_map/ppermute | solution.py:619
  216.5 6.6 %collective-permute-done.53 = bf16[256,768]{1,0:T(8,128)(2,1)S(1)} collective-permute-done((bf16[256,768]{1,0:T(8,128)(2,1)S(1)}, bf16[256,768]{1,0:T(8,128)(2,1)S(1)}, u32[]{:S(2)}, u32[]{:S(2)}) %collective-permute-start.53) | collective-permute-done | bytes 393248 | tf_op jit(solution)/shard_map/ppermute | solution.py:619
  227.1 8.5 %collective-permute-done.55 = bf16[256,768]{1,0:T(8,128)(2,1)S(1)} collective-permute-done((bf16[256,768]{1,0:T(8,128)(2,1)S(1)}, bf16[256,768]{1,0:T(8,128)(2,1)S(1)}, u32[]{:S(2)}, u32[]{:S(2)}) %collective-permute-start.55) | collective-permute-done | bytes 393248 | tf_op jit(solution)/shard_map/ppermute | solution.py:619
  256.6 2.9 %collective-permute-start.58 = (f32[8,1664]{1,0:T(8,128)S(1)}, f32[8,1664]{1,0:T(8,128)S(1)}, u32[]{:S(2)}, u32[]{:S(2)}) collective-permute-start(f32[8,1664]{1,0:T(8,128)S(1)} %add.219), channel_id=1, source_target_pairs={{0,8},{4,12},{8,0},{12,4},{1,9},{5,13},{9,1},{13,5},{2,10},{6,14},... | collective-permute-start | bytes 159752 | tf_op jit(solution)/shard_map/ppermute | solution.py:619
  260.7 3.5 %collective-permute-done.58 = f32[8,1664]{1,0:T(8,128)S(1)} collective-permute-done((f32[8,1664]{1,0:T(8,128)S(1)}, f32[8,1664]{1,0:T(8,128)S(1)}, u32[]{:S(2)}, u32[]{:S(2)}) %collective-permute-start.58) | collective-permute-done | bytes 53280 | tf_op jit(solution)/shard_map/ppermute | solution.py:619
  (308 shorter events, 139.2 us)
Async XLA Ops:
  3.5 15.1 %collective-permute-start = (bf16[128,896]{1,0:T(8,128)(2,1)S(1)}, bf16[128,896]{1,0:T(8,128)(2,1)S(1)}, u32[]{:S(2)}, u32[]{:S(2)}) collective-permute-start(bf16[128,896]{1,0:T(8,128)(2,1)S(1)} %concatenate.37.refs_7_), channel_id=1, source_target_pairs={{0,8},{4,12},{8,0},{12,4},{1,9},{5,13},{9,1},{13,5},{2,10},{6,14},... | collective-permute-start | bytes 688136 | tf_op jit(solution)/shard_map/ppermute | solution.py:619
  18.6 21.1 %collective-permute-start.5 = (bf16[128,1536]{1,0:T(8,128)(2,1)S(1)}, bf16[128,1536]{1,0:T(8,128)(2,1)S(1)}, u32[]{:S(2)}, u32[]{:S(2)}) collective-permute-start(bf16[128,1536]{1,0:T(8,128)(2,1)S(1)} %pad_maximum_fusion.1.refs_6_), channel_id=1, source_target_pairs={{0,8},{4,12},{8,0},{12,4},{1,9},{5,13},{9,1},{13,5},{2,10},{6,14},... | collective-permute-start | bytes 1179656 | tf_op jit(solution)/shard_map/ppermute | solution.py:619
  42.0 21.9 %collective-permute-start.11 = (bf16[128,1536]{1,0:T(8,128)(2,1)S(1)}, bf16[128,1536]{1,0:T(8,128)(2,1)}, u32[]{:S(2)}, u32[]{:S(2)}) collective-permute-start(bf16[128,1536]{1,0:T(8,128)(2,1)S(1)} %pad_maximum_fusion.1.refs_6_), channel_id=1, source_target_pairs={{0,4},{4,0},{8,12},{12,8},{1,5},{5,1},{9,13},{13,9},{2,6},{6,2},{1... | collective-permute-start | bytes 1179656 | tf_op jit(solution)/shard_map/ppermute | solution.py:619
  42.1 21.8 %collective-permute-start.13 = (bf16[128,1536]{1,0:T(8,128)(2,1)S(1)}, bf16[128,1536]{1,0:T(8,128)(2,1)}, u32[]{:S(2)}, u32[]{:S(2)}) collective-permute-start(bf16[128,1536]{1,0:T(8,128)(2,1)S(1)} %pad_maximum_fusion.1.refs_6_), channel_id=1, source_target_pairs={{0,16},{16,0},{1,17},{17,1},{2,18},{18,2},{3,19},{19,3},{4,20},{20... | collective-permute-start | bytes 1179656 | tf_op jit(solution)/shard_map/ppermute | solution.py:619
  42.7 21.2 %collective-permute-start.10 = (bf16[128,1024]{1,0:T(8,128)(2,1)S(1)}, bf16[128,1024]{1,0:T(8,128)(2,1)S(1)}, u32[]{:S(2)}, u32[]{:S(2)}) collective-permute-start(bf16[128,1024]{1,0:T(8,128)(2,1)S(1)} %pad_maximum_fusion.2.refs_2_), channel_id=1, source_target_pairs={{0,4},{4,0},{8,12},{12,8},{1,5},{5,1},{9,13},{13,9},{2,6},{6,2},{1... | collective-permute-start | bytes 786440 | tf_op jit(solution)/shard_map/ppermute | solution.py:619
  44.7 19.2 %collective-permute-start.12 = (bf16[128,1024]{1,0:T(8,128)(2,1)S(1)}, bf16[128,1024]{1,0:T(8,128)(2,1)S(1)}, u32[]{:S(2)}, u32[]{:S(2)}) collective-permute-start(bf16[128,1024]{1,0:T(8,128)(2,1)S(1)} %pad_maximum_fusion.2.refs_2_), channel_id=1, source_target_pairs={{0,16},{16,0},{1,17},{17,1},{2,18},{18,2},{3,19},{19,3},{4,20},{20... | collective-permute-start | bytes 786440 | tf_op jit(solution)/shard_map/ppermute | solution.py:619
  49.0 14.9 %collective-permute-start.9 = (bf16[128,1024]{1,0:T(8,128)(2,1)S(1)}, bf16[128,1024]{1,0:T(8,128)(2,1)S(1)}, u32[]{:S(2)}, u32[]{:S(2)}) collective-permute-start(bf16[128,1024]{1,0:T(8,128)(2,1)S(1)} %pad_maximum_fusion.2.refs_2_), channel_id=1, source_target_pairs={{0,8},{4,12},{8,0},{12,4},{1,9},{5,13},{9,1},{13,5},{2,10},{6,14},... | collective-permute-start | bytes 786440 | tf_op jit(solution)/shard_map/ppermute | solution.py:619
  77.3 17.9 %collective-permute-start.17 = (bf16[128,1536]{1,0:T(8,128)(2,1)S(1)}, bf16[128,1536]{1,0:T(8,128)(2,1)S(1)}, u32[]{:S(2)}, u32[]{:S(2)}) collective-permute-start(bf16[128,1536]{1,0:T(8,128)(2,1)S(1)} %copy-done.25), channel_id=1, source_target_pairs={{0,16},{16,0},{1,17},{17,1},{2,18},{18,2},{3,19},{19,3},{4,20},{20... | collective-permute-start | bytes 1179656 | tf_op jit(solution)/shard_map/ppermute | solution.py:619
  77.9 17.3 %collective-permute-start.18 = (bf16[128,1024]{1,0:T(8,128)(2,1)S(1)}, bf16[128,1024]{1,0:T(8,128)(2,1)S(1)}, u32[]{:S(2)}, u32[]{:S(2)}) collective-permute-start(bf16[128,1024]{1,0:T(8,128)(2,1)S(1)} %collective-permute-done.14.refs_5_), channel_id=1, source_target_pairs={{0,16},{16,0},{1,17},{17,1},{2,18},{18,2},{3,19},{19,3},{4,20},{20... | collective-permute-start | bytes 786440 | tf_op jit(solution)/shard_map/ppermute | solution.py:619
  95.2 14.0 %collective-permute-start.24 = (bf16[128,1536]{1,0:T(8,128)(2,1)S(1)}, bf16[128,1536]{1,0:T(8,128)(2,1)S(1)}, u32[]{:S(2)}, u32[]{:S(2)}) collective-permute-start(bf16[128,1536]{1,0:T(8,128)(2,1)S(1)} %copy-done.25), channel_id=1, source_target_pairs={{0,4},{4,0},{8,12},{12,8},{1,5},{5,1},{9,13},{13,9},{2,6},{6,2},{1... | collective-permute-start | bytes 1179656 | tf_op jit(solution)/shard_map/ppermute | solution.py:619
  131.4 19.7 %collective-permute-start.35 = (bf16[256,1536]{1,0:T(8,128)(2,1)S(1)}, bf16[256,1536]{1,0:T(8,128)(2,1)S(1)}, u32[]{:S(2)}, u32[]{:S(2)}) collective-permute-start(bf16[256,1536]{1,0:T(8,128)(2,1)S(1)} %get-tuple-element.291), channel_id=1, source_target_pairs={{0,16},{16,0},{1,17},{17,1},{2,18},{18,2},{3,19},{19,3},{4,20},{20... | collective-permute-start | bytes 2359304 | tf_op jit(solution)/shard_map/ppermute | solution.py:619
  153.4 21.6 %collective-permute-start.39 = (bf16[256,1024]{1,0:T(8,128)(2,1)S(1)}, bf16[256,1024]{1,0:T(8,128)(2,1)S(1)}, u32[]{:S(2)}, u32[]{:S(2)}) collective-permute-start(bf16[256,1024]{1,0:T(8,128)(2,1)S(1)} %get-tuple-element.293), channel_id=1, source_target_pairs={{0,16},{16,0},{1,17},{17,1},{2,18},{18,2},{3,19},{19,3},{4,20},{20... | collective-permute-start | bytes 1572872 | tf_op jit(solution)/shard_map/ppermute | solution.py:619
  156.2 18.7 %collective-permute-start.37 = (bf16[224,384]{1,0:T(8,128)(2,1)S(1)}, bf16[224,384]{1,0:T(8,128)(2,1)S(1)}, u32[]{:S(2)}, u32[]{:S(2)}) collective-permute-start(bf16[224,384]{1,0:T(8,128)(2,1)S(1)} %get-tuple-element.216), channel_id=1, source_target_pairs={{8,0},{12,4},{9,1},{13,5},{10,2},{14,6},{11,3},{15,7},{24,16},{28,... | collective-permute-start | bytes 516104 | tf_op jit(solution)/shard_map/ppermute | solution.py:619
  157.5 17.4 %collective-permute-start.38 = (bf16[224,384]{1,0:T(8,128)(2,1)S(1)}, bf16[224,384]{1,0:T(8,128)(2,1)S(1)}, u32[]{:S(2)}, u32[]{:S(2)}) collective-permute-start(bf16[224,384]{1,0:T(8,128)(2,1)S(1)} %get-tuple-element.217), channel_id=1, source_target_pairs={{12,0},{13,1},{14,2},{15,3},{28,16},{29,17},{30,18},{31,19}} | collective-permute-start | bytes 516104 | tf_op jit(solution)/shard_map/ppermute | solution.py:619
  158.8 35.9 %collective-permute-start.41 = (bf16[256,1536]{1,0:T(8,128)(2,1)S(1)}, bf16[256,1536]{1,0:T(8,128)(2,1)S(1)}, u32[]{:S(2)}, u32[]{:S(2)}) collective-permute-start(bf16[256,1536]{1,0:T(8,128)(2,1)S(1)} %get-tuple-element.241), channel_id=1, source_target_pairs={{0,16},{16,0},{1,17},{17,1},{2,18},{18,2},{3,19},{19,3},{4,20},{20... | collective-permute-start | bytes 2359304 | tf_op jit(solution)/shard_map/ppermute | solution.py:619
  175.2 19.6 %collective-permute-start.43 = (bf16[256,1536]{1,0:T(8,128)(2,1)S(1)}, bf16[256,1536]{1,0:T(8,128)(2,1)S(1)}, u32[]{:S(2)}, u32[]{:S(2)}) collective-permute-start(bf16[256,1536]{1,0:T(8,128)(2,1)S(1)} %add_convert_fusion), channel_id=1, source_target_pairs={{0,4},{4,0},{8,12},{12,8},{1,5},{5,1},{9,13},{13,9},{2,6},{6,2},{1... | collective-permute-start | bytes 2359304 | tf_op jit(solution)/shard_map/ppermute | solution.py:619
  175.3 19.5 %collective-permute-start.42 = (bf16[256,1024]{1,0:T(8,128)(2,1)S(1)}, bf16[256,1024]{1,0:T(8,128)(2,1)S(1)}, u32[]{:S(2)}, u32[]{:S(2)}) collective-permute-start(bf16[256,1024]{1,0:T(8,128)(2,1)S(1)} %get-tuple-element.292), channel_id=1, source_target_pairs={{0,16},{16,0},{1,17},{17,1},{2,18},{18,2},{3,19},{19,3},{4,20},{20... | collective-permute-start | bytes 1572872 | tf_op jit(solution)/shard_map/ppermute | solution.py:619
  206.9 20.2 %collective-permute-start.63 = (bf16[128,1536]{1,0:T(8,128)(2,1)S(1)}, bf16[128,1536]{1,0:T(8,128)(2,1)S(1)}, u32[]{:S(2)}, u32[]{:S(2)}) collective-permute-start(bf16[128,1536]{1,0:T(8,128)(2,1)S(1)} %slice.239), channel_id=1, source_target_pairs={{0,8},{4,12},{8,0},{12,4},{1,9},{5,13},{9,1},{13,5},{2,10},{6,14},... | collective-permute-start | bytes 1179656 | tf_op jit(solution)/shard_map/ppermute | solution.py:619
  216.1 19.5 %collective-permute-start.55 = (bf16[256,768]{1,0:T(8,128)(2,1)S(1)}, bf16[256,768]{1,0:T(8,128)(2,1)S(1)}, u32[]{:S(2)}, u32[]{:S(2)}) collective-permute-start(bf16[256,768]{1,0:T(8,128)(2,1)S(1)} %add_convert_fusion.2), channel_id=1, source_target_pairs={{0,4},{4,0},{8,12},{12,8},{1,5},{5,1},{9,13},{13,9},{2,6},{6,2},{1... | collective-permute-start | bytes 1179656 | tf_op jit(solution)/shard_map/ppermute | solution.py:619
  224.0 25.5 %collective-permute-start.59 = (bf16[256,1024]{1,0:T(8,128)(2,1)}, bf16[256,1024]{1,0:T(8,128)(2,1)}, u32[]{:S(2)}, u32[]{:S(2)}) collective-permute-start(bf16[256,1024]{1,0:T(8,128)(2,1)} %add_convert_fusion.1), channel_id=1, source_target_pairs={{0,4},{4,0},{8,12},{12,8},{1,5},{5,1},{9,13},{13,9},{2,6},{6,2},{1... | collective-permute-start | bytes 1572872 | tf_op jit(solution)/shard_map/ppermute | solution.py:619
  224.4 19.6 %collective-permute-start.49 = (bf16[128,1024]{1,0:T(8,128)(2,1)S(1)}, bf16[128,1024]{1,0:T(8,128)(2,1)}, u32[]{:S(2)}, u32[]{:S(2)}) collective-permute-start(bf16[128,1024]{1,0:T(8,128)(2,1)S(1)} %add_convert_fusion.5.refs_1_), channel_id=1, source_target_pairs={{0,1},{1,0},{2,3},{3,2},{4,5},{5,4},{6,7},{7,6},{8,9},{9,8},{10,11... | collective-permute-start | bytes 786440 | tf_op jit(solution)/shard_map/ppermute | solution.py:619
  224.4 16.2 %collective-permute-start.46 = (bf16[128,1024]{1,0:T(8,128)(2,1)}, bf16[128,1024]{1,0:T(8,128)(2,1)}, u32[]{:S(2)}, u32[]{:S(2)}) collective-permute-start(bf16[128,1024]{1,0:T(8,128)(2,1)} %get-tuple-element.254), channel_id=1, source_target_pairs={{0,1},{1,0},{2,3},{3,2},{4,5},{5,4},{6,7},{7,6},{8,9},{9,8},{10,11... | collective-permute-start | bytes 786440 | tf_op jit(solution)/shard_map/ppermute | solution.py:619
  242.5 17.0 %collective-permute-start.47 = (bf16[128,1024]{1,0:T(8,128)(2,1)}, bf16[128,1024]{1,0:T(8,128)(2,1)}, u32[]{:S(2)}, u32[]{:S(2)}) collective-permute-start(bf16[128,1024]{1,0:T(8,128)(2,1)} %add_convert_fusion.4), channel_id=1, source_target_pairs={{0,2},{1,3},{2,0},{3,1},{4,6},{5,7},{6,4},{7,5},{8,10},{9,11},{10,... | collective-permute-start | bytes 786440 | tf_op jit(solution)/shard_map/ppermute | solution.py:619
  251.8 17.4 %collective-permute-start.60 = (bf16[128,1024]{1,0:T(8,128)(2,1)S(1)}, bf16[128,1024]{1,0:T(8,128)(2,1)}, u32[]{:S(2)}, u32[]{:S(2)}) collective-permute-start(bf16[128,1024]{1,0:T(8,128)(2,1)S(1)} %slice.240), channel_id=1, source_target_pairs={{0,8},{4,12},{8,0},{12,4},{1,9},{5,13},{9,1},{13,5},{2,10},{6,14},... | collective-permute-start | bytes 786440 | tf_op jit(solution)/shard_map/ppermute | solution.py:619
  (89 other events, 916.0 us)
